TPU v7x, 128 devices: a whole 4x4x4 slice. The times are simulated.
128 devices in a mesh: head: 4 (over z), tok: 32 (over y, x, core).
Axes of the slice: x: 4, y: 4, z: 4, core: 2. Of those that a mesh axis runs over, the one named last changes fastest.
Arguments:
- query_tokens: bfloat16 [16384, 2048], P(('head', 'tok')), may hold values from -6 to 6
- key_tokens: bfloat16 [16384, 2048], P(('head', 'tok')), may hold values from -6 to 6
- value_tokens: bfloat16 [16384, 2048], P(('head', 'tok')), may hold values from -6 to 6
- step_sizes: bfloat16 [16384, 8], P(('head', 'tok')), may hold values from 0.00049972534 to 0.0049743652
- fast_weights: float32 [8, 3, 512, 256], P('head'), may hold values from -0.375 to 0.375
- out_grad: bfloat16 [16384, 2048], P(('head', 'tok')), may hold values from -6 to 6
Outputs:
- meta_grad: float32 [8, 3, 512, 256], P('head', None, 'tok')
- query_grad: bfloat16 [16384, 2048], P(('head', 'tok'))
- key_grad: bfloat16 [16384, 2048], P(('head', 'tok'))
- value_grad: bfloat16 [16384, 2048], P(('head', 'tok'))
- step_grad: bfloat16 [16384, 8], P(('head', 'tok'))
All inputs are finite; a program needn't handle non-finite values.
Results may differ from a plain program's by a relative error of at most 0.006.
Values may be sent and summed in bfloat16 or wider, within the bound.
No kernel may reach another device: no remote copies, remote signals or barrier semaphores. Data moves between devices by JAX's collectives and lax.ppermute only.
A program may use at most 128 MiB of HBM per device.

v0:
```python
import functools

import jax
import jax.numpy as jnp
from jax import lax
from jax.experimental import pallas as pl
from jax.experimental.pallas import tpu as pltpu
from jax.sharding import Mesh
from jax.sharding import PartitionSpec as P

EPSILON = 1e-05
PAD = 16
STEPS = 2
F32 = jnp.float32
BF16 = jnp.bfloat16


def mm(left, right, contract=(1, 0)):
    return lax.dot_general(
        left, right, (((contract[0],), (contract[1],)), ((), ())), preferred_element_type=F32
    )


def halves(value):
    high = value.astype(BF16)
    return high, (value - high.astype(F32)).astype(BF16)


def call(kernel, out_shape, flops=0, size=4 << 20, vmem=8, **options):
    return pl.pallas_call(
        kernel,
        out_shape=out_shape,
        compiler_params=pltpu.CompilerParams(vmem_limit_bytes=vmem << 20),
        cost_estimate=pl.CostEstimate(flops=flops, bytes_accessed=size, transcendentals=0),
        **options,
    )


def shape(dims, dtype):
    return jax.ShapeDtypeStruct(dims, dtype)


def mask_row(dims, index):
    return lax.broadcasted_iota(jnp.int32, dims, 0) == index


def padded_row(row, width):
    block = jnp.broadcast_to(row, (PAD, row.shape[1]))
    return jnp.concatenate([block] * (width // row.shape[1]), axis=1).astype(BF16)


def columns_of(place_ref, slot, width):
    return pl.ds(pl.multiple_of(place_ref[slot] * width, width), width)


def pieces(own_refs, got_refs):
    half = own_refs[0].shape[0] // 2
    return [ref.at[:half] for ref in own_refs] + [ref.at[half:] for ref in got_refs]


def pack_kv_kernel(place_ref, key_ref, value_ref, rate_ref, *out_refs):
    rows, width = key_ref.shape[0], out_refs[0].shape[1]
    rates = rate_ref[...].astype(F32)
    for slot, out_ref in enumerate(pieces(out_refs, out_refs)):
        columns = columns_of(place_ref, slot, width)
        out_ref[:rows] = key_ref[:, columns]
        out_ref[rows : 2 * rows] = value_ref[:, columns]
        chosen = jnp.where(mask_row(rates.shape, place_ref[slot]), rates, 0.0)
        out_ref[2 * rows :] = padded_row(jnp.sum(chosen, axis=0, keepdims=True), width)


def pack_qg_kernel(place_ref, query_ref, cotangent_ref, *out_refs):
    rows, width = query_ref.shape[0], out_refs[0].shape[1]
    for slot, out_ref in enumerate(pieces(out_refs, out_refs)):
        columns = columns_of(place_ref, slot, width)
        out_ref[:rows] = query_ref[:, columns]
        out_ref[rows:] = cotangent_ref[:, columns]


def unpack_kv_kernel(place_ref, *refs):
    in_refs, (key_ref, value_ref, rate_ref) = refs[:-3], refs[-3:]
    rows, width = key_ref.shape[0], in_refs[0].shape[1]
    count = len(in_refs) // 2
    rates = jnp.zeros(rate_ref.shape, F32)
    for slot, in_ref in enumerate(pieces(in_refs[:count], in_refs[count:])):
        columns = columns_of(place_ref, slot, width)
        key_ref[:, columns] = in_ref[:rows]
        value_ref[:, columns] = in_ref[rows : 2 * rows]
        row = in_ref[2 * rows :, :rows].astype(F32)[:1]
        rates = jnp.where(mask_row(rates.shape, place_ref[slot]), row, rates)
    rate_ref[...] = rates.astype(BF16)


def unpack_q_kernel(place_ref, *refs):
    in_refs, query_ref = refs[:-1], refs[-1]
    width, count = in_refs[0].shape[1], len(in_refs) // 2
    for slot, in_ref in enumerate(pieces(in_refs[:count], in_refs[count:])):
        query_ref[:, columns_of(place_ref, slot, width)] = in_ref[...]


def rows_of(refs, start, count):
    return jnp.concatenate([ref[start : start + count] for ref in refs], axis=0)


def rate_row(refs, rows):
    return jnp.concatenate([ref[2 * rows :, :rows].astype(F32)[:1] for ref in refs], axis=1)


def groups_of(refs):
    size = len(refs) // STEPS
    return [(step, refs[step * size : (step + 1) * size]) for step in range(STEPS)]


def start_all(pairs, sem_ref, first=0):
    copies = [
        pltpu.make_async_copy(source, target, sem_ref.at[first + number])
        for number, (source, target) in enumerate(pairs)
    ]
    for copy in copies:
        copy.start()
    return copies


def add_to(acc_ref, out_ref, step, index, value):
    owners, _, share, width = out_ref.shape
    if step:
        value = acc_ref[index] + value
    if step < STEPS - 1:
        acc_ref[index] = value
    else:
        out_ref[:, index] = value.astype(BF16).reshape(owners, share, width)


def inner_kernel(rows, *refs):
    sources, (wh_ref, wl_ref, act_ref, out_ref, acc_ref, held_ref, sem_ref) = refs[:-7], refs[-7:]
    messages = pieces(sources[: len(sources) // 2], sources[len(sources) // 2 :])
    copies = []
    for step, group in groups_of(messages):
        put = functools.partial(add_to, acc_ref, out_ref, step)
        k, v = rows_of(group, 0, rows), rows_of(group, rows, rows)
        r = rate_row(group, rows)
        a = mm(wh_ref[0], k, (1, 1)) + mm(wl_ref[0], k, (1, 1))
        b = mm(wh_ref[1], k, (1, 1)) + mm(wl_ref[1], k, (1, 1))
        d = mm(wh_ref[2], v, (1, 1)) + mm(wl_ref[2], v, (1, 1))
        held_ref[step, 0], held_ref[step, 1], held_ref[step, 2] = a, b, d
        copies += start_all([(held_ref.at[step], act_ref.at[step])], sem_ref, step)
        s = jax.nn.sigmoid(a)
        sa = a * s
        dh = d * r
        hid_h, hid_l = halves(sa * b * r)
        put(2, mm(hid_h, v) + mm(hid_l, v))
        du_h, du_l = halves(dh * sa)
        put(1, mm(du_h, k) + mm(du_l, k))
        dg_h, dg_l = halves(dh * b * (s * (1.0 + a * (1.0 - s))))
        put(0, mm(dg_h, k) + mm(dg_l, k))
    for copy in copies:
        copy.wait()


def whole(ref, index):
    part = ref[:, index]
    return part.reshape(part.shape[0] * part.shape[1], part.shape[2])


def give(refs, value, start, rows):
    rounded = value.T.astype(BF16)
    for slot, ref in enumerate(refs):
        ref[start : start + rows] = rounded[slot * rows : (slot + 1) * rows]


def outer_kernel(rows, *refs):
    layers = (len(refs) - 5) // 3
    messages, n_ref = pieces(refs[:layers], refs[layers : 2 * layers]), refs[2 * layers]
    gifts, (out_ref, acc_ref, held_ref, sem_ref) = refs[2 * layers + 1 : -4], refs[-4:]
    gifts = pieces(gifts, gifts)
    copies = []
    gate, up, down = whole(n_ref, 0), whole(n_ref, 1), whole(n_ref, 2)
    for (step, group), (_, back) in zip(groups_of(messages), groups_of(gifts)):
        put = functools.partial(add_to, acc_ref, out_ref, step)
        q, g = rows_of(group, 0, rows), rows_of(group, rows, rows)
        a, b, d = mm(gate, q, (1, 1)), mm(up, q, (1, 1)), mm(down, g, (1, 1))
        s = jax.nn.sigmoid(a)
        sa = a * s
        hid_h, hid_l = halves(sa * b)
        put(2, mm(hid_h, g) + mm(hid_l, g))
        du_h, du_l = halves(d * sa)
        put(1, mm(du_h, q) + mm(du_l, q))
        dg_h, dg_l = halves(d * b * (s * (1.0 + a * (1.0 - s))))
        put(0, mm(dg_h, q) + mm(dg_l, q))
        dq = mm(gate, dg_h, (0, 0)) + mm(gate, dg_l, (0, 0))
        dq += mm(up, du_h, (0, 0)) + mm(up, du_l, (0, 0))
        held = [held_ref.at[step * len(back) + slot] for slot in range(len(back))]
        give(held, dq, 0, rows)
        copies += start_all(list(zip(held, back)), sem_ref, step * len(back))
    for copy in copies:
        copy.wait()


def second_kernel(rows, *refs):
    layers = (len(refs) - 12) // 3
    sources = pieces(refs[:layers], refs[layers : 2 * layers])
    wh_ref, wl_ref, c_ref, stored_ref = refs[2 * layers : 2 * layers + 4]
    gifts, rest = refs[2 * layers + 4 : -8], refs[-8:]
    gifts = pieces(gifts, gifts)
    out_ref, acc_ref, message_ref, act_ref, held_ref, message_sem, act_sem, held_sem = rest
    messages = [message_ref.at[slot] for slot in range(len(sources))]
    loads = start_all(list(zip(sources, messages)), message_sem)
    act_loads = start_all([(stored_ref.at[step], act_ref.at[step]) for step in range(STEPS)], act_sem)
    copies = []
    gate, up, down = whole(c_ref, 0), whole(c_ref, 1), whole(c_ref, 2)
    for (step, group), (_, back) in zip(groups_of(messages), groups_of(gifts)):
        put = functools.partial(add_to, acc_ref, out_ref, step)
        for load in loads[step * len(group) : (step + 1) * len(group)]:
            load.wait()
        k, v = rows_of(group, 0, rows), rows_of(group, rows, rows)
        r = rate_row(group, rows)
        big_a, big_b, e = mm(gate, k, (1, 1)), mm(up, k, (1, 1)), mm(down, v, (1, 1))
        act_loads[step].wait()
        a, b, d = act_ref[step, 0], act_ref[step, 1], act_ref[step, 2]
        s = jax.nn.sigmoid(a)
        sa = a * s
        ds = s * (1.0 + a * (1.0 - s))
        dds = s * (1.0 - s) * (2.0 + a * (1.0 - 2.0 * s))
        dh, er = d * r, e * r
        bds = b * ds
        hid = sa * b
        ddh = big_a * bds + big_b * sa
        d_rate = jnp.sum(hid * e + ddh * d, axis=0, keepdims=True)
        db_h, db_l = halves(er * sa + big_a * (dh * ds))
        da_h, da_l = halves((er * b + big_b * dh) * ds + big_a * (dh * b * dds))
        put(0, mm(da_h, k) + mm(da_l, k))
        put(1, mm(db_h, k) + mm(db_l, k))
        dr_h, dr_l = halves(ddh * r)
        put(2, mm(dr_h, v) + mm(dr_l, v))
        hid_h, hid_l = halves(hid * r)
        dv = mm(down, hid_h, (0, 0)) + mm(down, hid_l, (0, 0))
        dv += mm(wh_ref[2], dr_h, (0, 0)) + mm(wh_ref[2], dr_l, (0, 0)) + mm(wl_ref[2], dr_h, (0, 0))
        dg_h, dg_l = halves(dh * bds)
        du_h, du_l = halves(dh * sa)
        dk = mm(gate, dg_h, (0, 0)) + mm(gate, dg_l, (0, 0))
        dk += mm(up, du_h, (0, 0)) + mm(up, du_l, (0, 0))
        dk += mm(wh_ref[0], da_h, (0, 0)) + mm(wh_ref[0], da_l, (0, 0)) + mm(wl_ref[0], da_h, (0, 0))
        dk += mm(wh_ref[1], db_h, (0, 0)) + mm(wh_ref[1], db_l, (0, 0)) + mm(wl_ref[1], db_h, (0, 0))
        held = [held_ref.at[step * len(back) + slot] for slot in range(len(back))]
        give(held, dk, 0, rows)
        give(held, dv, rows, rows)
        for slot, ref in enumerate(held):
            ref[2 * rows :] = padded_row(d_rate[:, slot * rows : (slot + 1) * rows], ref.shape[1])
        copies += start_all(list(zip(held, back)), held_sem, step * len(back))
    for copy in copies:
        copy.wait()


def total_of(in_ref):
    total = in_ref[0].astype(F32)
    for source in range(1, in_ref.shape[0]):
        total += in_ref[source].astype(F32)
    return total


def norm_of(rows):
    return jnp.sqrt(jnp.sum(rows * rows, axis=-1, keepdims=True) + EPSILON)


def spread(value, out_ref):
    rounded = value.astype(BF16)
    for owner in range(out_ref.shape[0]):
        out_ref[owner] = rounded


def update_kernel(in_ref, w_ref, out_ref, moved_ref):
    w = w_ref[...]
    moved = w + total_of(in_ref)
    moved_ref[...] = moved
    spread(moved * (norm_of(w) / norm_of(moved)), out_ref)


def back_kernel(in_ref, w_ref, moved_ref, out_ref, direct_ref):
    w, moved = w_ref[...], moved_ref[...]
    given = total_of(in_ref)
    old, new = norm_of(w), norm_of(moved)
    along = jnp.sum(given * moved, axis=-1, keepdims=True) / new
    cotangent = (given - moved * (along / new)) * (old / new)
    direct_ref[...] = cotangent + w * (along / old)
    spread(cotangent, out_ref)


def last_kernel(in_ref, direct_ref, out_ref):
    out_ref[...] = total_of(in_ref) + direct_ref[...]


def body(query_tokens, key_tokens, value_tokens, step_sizes, fast_weights, out_grad):
    rows = query_tokens.shape[0]
    layers, cores = lax.axis_size("z"), lax.axis_size("c")
    heads = layers * cores
    owners = lax.axis_size("p")
    width = query_tokens.shape[1] // heads
    hid = fast_weights.shape[2]
    share = hid // owners
    layer, place, core = lax.axis_index("z"), lax.axis_index("p"), lax.axis_index("c")
    product = 2 * heads * rows * hid * width
    shifts = [0, layers // 2] + [up for up in range(1, layers) if up != layers // 2]
    places = jnp.stack(
        [(layer + up) % layers * cores + (core + over) % cores for over in range(cores) for up in shifts]
    ).astype(jnp.int32)

    def along(messages, sign):
        pairs = [[(z, (z + sign * up) % layers) for z in range(layers)] for up in shifts]
        moved = [lax.ppermute(m, "z", pair) for m, pair in zip(messages[1:], pairs[1:])]
        return [messages[0]] + moved

    def across(messages):
        return [lax.ppermute(message, "c", [(0, 1), (1, 0)]) for message in messages]

    def scatter(message):
        message = message.reshape(owners, 3 * share, width)
        return lax.all_to_all(message, "p", 0, 0, tiled=True)

    weights = lax.dynamic_index_in_dim(fast_weights, core, 0, keepdims=False)
    own = lax.dynamic_slice_in_dim(weights, place * share, share, 1).reshape(3 * share, width)
    rounded = lax.reduce_precision(weights, 8, 7)
    w_high, w_low = rounded.astype(BF16), (weights - rounded).astype(BF16)
    memory = pl.BlockSpec(memory_space=pltpu.VMEM)
    scalars = pl.BlockSpec(memory_space=pltpu.SMEM)

    def messages_of(count):
        return (shape((cores * count, width), BF16),) * layers

    kv = along(
        call(
            pack_kv_kernel, messages_of(2 * rows + PAD), in_specs=[scalars, memory, memory, memory]
        )(places, key_tokens, value_tokens, step_sizes.T),
        1,
    )
    kv += across(kv)
    qg = along(
        call(pack_qg_kernel, messages_of(2 * rows), in_specs=[scalars, memory, memory])(
            places, query_tokens, out_grad
        ),
        1,
    )
    part_shape = shape((owners, 3, share, width), BF16)
    act_dims = (STEPS, 3, hid, heads * rows // STEPS)
    scratch = [pltpu.VMEM((3, hid, width), F32)]
    main = pl.BlockSpec(memory_space=pltpu.HBM)
    acts, grad_part = call(
        functools.partial(inner_kernel, rows),
        (shape(act_dims, F32), part_shape),
        flops=12 * product,
        vmem=60,
        in_specs=[memory] * (heads + 2),
        out_specs=[main, memory],
        scratch_shapes=scratch + [pltpu.VMEM(act_dims, F32), pltpu.SemaphoreType.DMA((STEPS,))],
    )(*kv, w_high, w_low)
    own_shape = shape((3 * share, width), F32)
    spread_shape = shape((owners, 3 * share, width), BF16)
    summed, qg = lax.optimization_barrier((scatter(grad_part), qg))
    updated, moved = call(update_kernel, (spread_shape, own_shape))(summed, own)
    updated, got = lax.optimization_barrier((scatter(updated), across(qg)))
    updated, qg = updated.reshape(owners, 3, share, width), qg + got
    *d_queries, d_part = call(
        functools.partial(outer_kernel, rows),
        messages_of(rows) + (part_shape,),
        flops=13 * product,
        vmem=60,
        in_specs=[memory] * (heads + 1),
        out_specs=[main] * layers + [memory],
        scratch_shapes=scratch
        + [pltpu.VMEM((heads, rows, width), BF16), pltpu.SemaphoreType.DMA((heads,))],
    )(*qg, updated)
    given, d_queries = lax.optimization_barrier((scatter(d_part), along(d_queries, -1)))
    cotangent, direct = call(back_kernel, (spread_shape, own_shape))(given, own, moved)
    wide = (rows, heads * width)
    taken = [scalars] + [memory] * heads
    query_grad = call(unpack_q_kernel, shape(wide, BF16), in_specs=taken)(
        places, *d_queries, *across(d_queries)
    )
    cotangent, query_grad = lax.optimization_barrier((scatter(cotangent), query_grad))
    cotangent = cotangent.reshape(owners, 3, share, width)
    *d_kv, second_part = call(
        functools.partial(second_kernel, rows),
        messages_of(2 * rows + PAD) + (part_shape,),
        flops=24 * product,
        vmem=60,
        in_specs=[main] * heads + [memory] * 3 + [main],
        out_specs=[main] * layers + [memory],
        scratch_shapes=scratch
        + [
            pltpu.VMEM((heads, 2 * rows + PAD, width), BF16),
            pltpu.VMEM(act_dims, F32),
            pltpu.VMEM((heads, 2 * rows + PAD, width), BF16),
            pltpu.SemaphoreType.DMA((heads,)),
            pltpu.SemaphoreType.DMA((STEPS,)),
            pltpu.SemaphoreType.DMA((heads,)),
        ],
    )(*kv, w_high, w_low, cotangent, acts)
    d_kv = along(d_kv, -1)
    key_grad, value_grad, step_grad = call(
        unpack_kv_kernel,
        (shape(wide, BF16), shape(wide, BF16), shape((heads, rows), BF16)),
        in_specs=taken,
    )(places, *d_kv, *across(d_kv))
    step_grad = step_grad.T
    summed = call(last_kernel, own_shape)(scatter(second_part), direct)
    summed = summed.reshape(3, 2, share // 2, width)
    kept = lax.dynamic_index_in_dim(summed, core, 1, keepdims=False)
    sent = lax.dynamic_index_in_dim(summed, 1 - core, 1, keepdims=False)
    got = lax.ppermute(sent, "c", [(0, 1), (1, 0)])
    first = core == 0
    meta_grad = jnp.stack([jnp.where(first, kept, got), jnp.where(first, got, kept)])
    return meta_grad, query_grad, key_grad, value_grad, step_grad


def solution(mesh):
    layers, lines = mesh.devices.shape
    small = Mesh(mesh.devices.reshape(layers, lines // 2, 2), ("z", "p", "c"))
    rows = P(("z", "p", "c"), None)
    return jax.shard_map(
        body,
        mesh=small,
        in_specs=(rows, rows, rows, rows, P("z", None, None, None), rows),
        out_specs=(P("z", None, ("p", "c"), None), rows, rows, rows, rows),
        check_vma=False,
    )
```

profile of v0, /device:TPU:1, one launch (start us, length us, event | category | flops | bytes accessed | tf_op | source)
XLA Modules:
  0.0 165.0 jit_solution(5477460148353687621)
XLA Ops:
  4.2 4.5 %collective-permute-start = (bf16[544,256]{1,0:T(8,128)(2,1)S(1)}, bf16[544,256]{1,0:T(8,128)(2,1)S(1)}, u32[]{:S(2)}, u32[]{:S(2)}) collective-permute-start(bf16[544,256]{1,0:T(8,128)(2,1)S(1)} %get-tuple-element.50), channel_id=1, source_target_pairs={{0,64},{32,96},{64,0},{96,32},{1,65},{33,97},{65,1},{97,33},{2,66}... | collective-permute-start | bytes 835592 | tf_op jit(solution)/shard_map/ppermute | solution.py:309
  12.9 2.2 %collective-permute-done.refs_1_ = bf16[544,256]{1,0:T(8,128)(2,1)S(1)} collective-permute-done((bf16[544,256]{1,0:T(8,128)(2,1)S(1)}, bf16[544,256]{1,0:T(8,128)(2,1)S(1)}, u32[]{:S(2)}, u32[]{:S(2)}) %collective-permute-start) | collective-permute-done | bytes 278560 | tf_op jit(solution)/shard_map/ppermute | solution.py:309
  15.2 2.1 %collective-permute-start.4 = (bf16[544,256]{1,0:T(8,128)(2,1)S(1)}, bf16[544,256]{1,0:T(8,128)(2,1)S(1)}, u32[]{:S(2)}, u32[]{:S(2)}) collective-permute-start(bf16[544,256]{1,0:T(8,128)(2,1)S(1)} %collective-permute-done.refs_1_), channel_id=1, source_target_pairs={{0,1},{1,0},{2,3},{3,2},{4,5},{5,4},{6,7},{7,6},{8,9},{9,8},{10,11... | collective-permute-start | bytes 835592 | tf_op jit(solution)/shard_map/ppermute | solution.py:313
  17.2 4.6 %collective-permute-done.1.refs_2_ = bf16[544,256]{1,0:T(8,128)(2,1)S(1)} collective-permute-done((bf16[544,256]{1,0:T(8,128)(2,1)S(1)}, bf16[544,256]{1,0:T(8,128)(2,1)S(1)}, u32[]{:S(2)}, u32[]{:S(2)}) %collective-permute-start.1) | collective-permute-done | bytes 278560 | tf_op jit(solution)/shard_map/ppermute | solution.py:309
  23.1 2.9 %fusion = (bf16[3,512,256]{2,1,0:T(8,128)(2,1)}, bf16[3,512,256]{2,1,0:T(8,128)(2,1)}) fusion(f32[2,3,512,256]{3,2,1,0:T(8,128)} %param.10, s32[]{:T(128)S(6)} %select_n.82), kind=kLoop, calls=%fused_computation.2 | loop fusion | flops 1572864 | bytes 3145732 | tf_op jit(solution)/shard_map/convert_element_type | solution.py:322
  27.0 7.9 %shard_map.102 = (f32[2,3,512,512]{3,2,1,0:T(8,128)}, bf16[16,3,32,256]{3,2,1,0:T(8,128)(2,1)}) custom-call(bf16[544,256]{1,0:T(8,128)(2,1)} %copy-done.7, bf16[544,256]{1,0:T(8,128)(2,1)} %copy-done.11, bf16[544,256]{1,0:T(8,128)(2,1)} %copy-done.12, bf16[544,256]{1,0:T(8,128)(2,1)} %copy-done.13, bf16[544,256]{1,0:T(8,128)(2,1)} %copy-done.14, ...), custom_call_target="tpu_custom_call" | custom-call | flops 3221225472 | bytes 4194304 | tf_op jit(solution)/shard_map/pallas_call | solution.py:346
  34.9 6.8 %all-to-all-start = ((bf16[16,96,256]{2,1,0:T(8,128)(2,1)}), bf16[16,96,256]{2,1,0:T(8,128)(2,1)S(1)}, u32[]{:S(2)}, u32[]{:S(2)}) async-start(bf16[16,96,256]{2,1,0:T(8,128)(2,1)} %bitcast.40), calls=%async_computation | async-start | bytes 1572864 | tf_op jit(solution)/shard_map/all_to_all | solution.py:317
  47.9 3.6 %collective-permute-done.7.refs_1_ = bf16[512,256]{1,0:T(8,128)(2,1)S(1)} collective-permute-done((bf16[512,256]{1,0:T(8,128)(2,1)S(1)}, bf16[512,256]{1,0:T(8,128)(2,1)S(1)}, u32[]{:S(2)}, u32[]{:S(2)}) %collective-permute-start.7) | collective-permute-done | bytes 262176 | tf_op jit(solution)/shard_map/ppermute | solution.py:309
  51.6 6.3 %collective-permute-done.8.refs_2_ = bf16[512,256]{1,0:T(8,128)(2,1)S(1)} collective-permute-done((bf16[512,256]{1,0:T(8,128)(2,1)S(1)}, bf16[512,256]{1,0:T(8,128)(2,1)S(1)}, u32[]{:S(2)}, u32[]{:S(2)}) %collective-permute-start.8) | collective-permute-done | bytes 262176 | tf_op jit(solution)/shard_map/ppermute | solution.py:309
  59.0 6.7 %all-to-all-start.1 = ((bf16[16,96,256]{2,1,0:T(8,128)(2,1)}), bf16[16,96,256]{2,1,0:T(8,128)(2,1)S(1)}, u32[]{:S(2)}, u32[]{:S(2)}) async-start(bf16[16,96,256]{2,1,0:T(8,128)(2,1)} %get-tuple-element.63), calls=%async_computation.1 | async-start | bytes 1572864 | tf_op jit(solution)/shard_map/all_to_all | solution.py:317
  68.8 10.2 %all-to-all-done.1 = bf16[16,96,256]{2,1,0:T(8,128)(2,1)S(1)} async-done(((bf16[16,96,256]{2,1,0:T(8,128)(2,1)}), bf16[16,96,256]{2,1,0:T(8,128)(2,1)S(1)}, u32[]{:S(2)}, u32[]{:S(2)}) %all-to-all-start.1) | async-done | bytes 786464 | tf_op jit(solution)/shard_map/all_to_all | solution.py:317
  80.0 8.1 %shard_map.105 = (bf16[256,256]{1,0:T(8,128)(2,1)}, bf16[256,256]{1,0:T(8,128)(2,1)}, bf16[256,256]{1,0:T(8,128)(2,1)}, bf16[256,256]{1,0:T(8,128)(2,1)}, bf16[16,3,32,256]{3,2,1,0:T(8,128)(2,1)}) custom-call(bf16[512,256]{1,0:T(8,128)(2,1)} %copy-done.8, bf16[512,256]{1,0:T(8,128)(2,1)} %copy-done.18, bf16[512,256]{1,0:T(8,128)(2,1)} %copy-done.19, ...), custom_call_target="tpu_custom_call" | custom-call | flops 3489660928 | bytes 4194304 | tf_op jit(solution)/shard_map/pallas_call | solution.py:361
  88.1 3.8 %all-to-all-start.2 = ((bf16[16,96,256]{2,1,0:T(8,128)(2,1)}), bf16[16,96,256]{2,1,0:T(8,128)(2,1)S(1)}, u32[]{:S(2)}, u32[]{:S(2)}) async-start(bf16[16,96,256]{2,1,0:T(8,128)(2,1)} %bitcast.42), calls=%async_computation.2 | async-start | bytes 1572864 | tf_op jit(solution)/shard_map/all_to_all | solution.py:317
  95.2 2.3 %collective-permute-done.14.refs_1_ = bf16[256,256]{1,0:T(8,128)(2,1)S(1)} collective-permute-done((bf16[256,256]{1,0:T(8,128)(2,1)}, bf16[256,256]{1,0:T(8,128)(2,1)S(1)}, u32[]{:S(2)}, u32[]{:S(2)}) %collective-permute-start.14) | collective-permute-done | bytes 131104 | tf_op jit(solution)/shard_map/ppermute | solution.py:309
  99.5 2.4 %collective-permute-done.16.refs_3_ = bf16[256,256]{1,0:T(8,128)(2,1)S(1)} collective-permute-done((bf16[256,256]{1,0:T(8,128)(2,1)}, bf16[256,256]{1,0:T(8,128)(2,1)S(1)}, u32[]{:S(2)}, u32[]{:S(2)}) %collective-permute-start.16) | collective-permute-done | bytes 131104 | tf_op jit(solution)/shard_map/ppermute | solution.py:309
  101.9 2.5 %all-to-all-done.2.in_ref = bf16[16,96,256]{2,1,0:T(8,128)(2,1)S(1)} async-done(((bf16[16,96,256]{2,1,0:T(8,128)(2,1)}), bf16[16,96,256]{2,1,0:T(8,128)(2,1)S(1)}, u32[]{:S(2)}, u32[]{:S(2)}) %all-to-all-start.2) | async-done | bytes 786464 | tf_op jit(solution)/shard_map/all_to_all | solution.py:317
  105.6 4.0 %all-to-all-start.3 = ((bf16[16,96,256]{2,1,0:T(8,128)(2,1)}), bf16[16,96,256]{2,1,0:T(8,128)(2,1)S(1)}, u32[]{:S(2)}, u32[]{:S(2)}) async-start(bf16[16,96,256]{2,1,0:T(8,128)(2,1)} %get-tuple-element.76), calls=%async_computation.3 | async-start | bytes 1572864 | tf_op jit(solution)/shard_map/all_to_all | solution.py:317
  109.6 2.8 %collective-permute-start.17 = (bf16[256,256]{1,0:T(8,128)(2,1)S(1)}, bf16[256,256]{1,0:T(8,128)(2,1)S(1)}, u32[]{:S(2)}, u32[]{:S(2)}) collective-permute-start(bf16[256,256]{1,0:T(8,128)(2,1)S(1)} %copy-done.5), channel_id=1, source_target_pairs={{0,1},{1,0},{2,3},{3,2},{4,5},{5,4},{6,7},{7,6},{8,9},{9,8},{10,11... | collective-permute-start | bytes 393224 | tf_op jit(solution)/shard_map/ppermute | solution.py:313
  115.7 5.7 %all-to-all-done.3 = bf16[16,96,256]{2,1,0:T(8,128)(2,1)S(1)} async-done(((bf16[16,96,256]{2,1,0:T(8,128)(2,1)}), bf16[16,96,256]{2,1,0:T(8,128)(2,1)S(1)}, u32[]{:S(2)}, u32[]{:S(2)}) %all-to-all-start.3) | async-done | bytes 786464 | tf_op jit(solution)/shard_map/all_to_all | solution.py:317
  122.3 17.8 %shard_map.108 = (bf16[544,256]{1,0:T(8,128)(2,1)}, bf16[544,256]{1,0:T(8,128)(2,1)}, bf16[544,256]{1,0:T(8,128)(2,1)}, bf16[544,256]{1,0:T(8,128)(2,1)}, bf16[16,3,32,256]{3,2,1,0:T(8,128)(2,1)}) custom-call(bf16[544,256]{1,0:T(8,128)(2,1)} %copy-done.7, bf16[544,256]{1,0:T(8,128)(2,1)} %copy-done.11, bf16[544,256]{1,0:T(8,128)(2,1)} %copy-done.12, ...), custom_call_target="tpu_custom_call" | custom-call | flops 6442450944 | bytes 4194304 | tf_op jit(solution)/shard_map/pallas_call | solution.py:380
  140.1 3.6 %all-to-all-start.4 = ((bf16[16,96,256]{2,1,0:T(8,128)(2,1)}), bf16[16,96,256]{2,1,0:T(8,128)(2,1)S(1)}, u32[]{:S(2)}, u32[]{:S(2)}) async-start(bf16[16,96,256]{2,1,0:T(8,128)(2,1)} %bitcast.38), calls=%async_computation.4 | async-start | bytes 1572864 | tf_op jit(solution)/shard_map/all_to_all | solution.py:317
  146.6 4.2 %collective-permute-start.25 = (bf16[544,256]{1,0:T(8,128)(2,1)}, bf16[544,256]{1,0:T(8,128)(2,1)S(1)}, u32[]{:S(2)}, u32[]{:S(2)}) collective-permute-start(bf16[544,256]{1,0:T(8,128)(2,1)} %get-tuple-element.86.refs_0_), channel_id=1, source_target_pairs={{0,1},{1,0},{2,3},{3,2},{4,5},{5,4},{6,7},{7,6},{8,9},{9,8},{10,11... | collective-permute-start | bytes 835592 | tf_op jit(solution)/shard_map/ppermute | solution.py:313
  151.0 6.7 %collective-permute-start.26 = (bf16[544,256]{1,0:T(8,128)(2,1)S(1)}, bf16[544,256]{1,0:T(8,128)(2,1)S(1)}, u32[]{:S(2)}, u32[]{:S(2)}) collective-permute-start(bf16[544,256]{1,0:T(8,128)(2,1)S(1)} %collective-permute-done.22.refs_1_), channel_id=1, source_target_pairs={{0,1},{1,0},{2,3},{3,2},{4,5},{5,4},{6,7},{7,6},{8,9},{9,8},{10,11... | collective-permute-start | bytes 835592 | tf_op jit(solution)/shard_map/ppermute | solution.py:313
  157.7 2.4 %collective-permute-start.27 = (bf16[544,256]{1,0:T(8,128)(2,1)S(1)}, bf16[544,256]{1,0:T(8,128)(2,1)S(1)}, u32[]{:S(2)}, u32[]{:S(2)}) collective-permute-start(bf16[544,256]{1,0:T(8,128)(2,1)S(1)} %collective-permute-done.23.refs_2_), channel_id=1, source_target_pairs={{0,1},{1,0},{2,3},{3,2},{4,5},{5,4},{6,7},{7,6},{8,9},{9,8},{10,11... | collective-permute-start | bytes 835592 | tf_op jit(solution)/shard_map/ppermute | solution.py:313
  (110 shorter events, 39.9 us)
Async XLA Ops:
  4.2 10.9 %collective-permute-start = (bf16[544,256]{1,0:T(8,128)(2,1)S(1)}, bf16[544,256]{1,0:T(8,128)(2,1)S(1)}, u32[]{:S(2)}, u32[]{:S(2)}) collective-permute-start(bf16[544,256]{1,0:T(8,128)(2,1)S(1)} %get-tuple-element.50), channel_id=1, source_target_pairs={{0,64},{32,96},{64,0},{96,32},{1,65},{33,97},{65,1},{97,33},{2,66}... | collective-permute-start | bytes 835592 | tf_op jit(solution)/shard_map/ppermute | solution.py:309
  8.8 13.1 %collective-permute-start.1 = (bf16[544,256]{1,0:T(8,128)(2,1)S(1)}, bf16[544,256]{1,0:T(8,128)(2,1)S(1)}, u32[]{:S(2)}, u32[]{:S(2)}) collective-permute-start(bf16[544,256]{1,0:T(8,128)(2,1)S(1)} %get-tuple-element.51), channel_id=1, source_target_pairs={{0,32},{32,64},{64,96},{96,0},{1,33},{33,65},{65,97},{97,1},{2,34}... | collective-permute-start | bytes 835592 | tf_op jit(solution)/shard_map/ppermute | solution.py:309
  9.5 12.8 %collective-permute-start.2 = (bf16[544,256]{1,0:T(8,128)(2,1)S(1)}, bf16[544,256]{1,0:T(8,128)(2,1)S(1)}, u32[]{:S(2)}, u32[]{:S(2)}) collective-permute-start(bf16[544,256]{1,0:T(8,128)(2,1)S(1)} %get-tuple-element.52), channel_id=1, source_target_pairs={{0,96},{32,0},{64,32},{96,64},{1,97},{33,1},{65,33},{97,65},{2,98}... | collective-permute-start | bytes 835592 | tf_op jit(solution)/shard_map/ppermute | solution.py:309
  11.4 14.5 %collective-permute-start.3 = (bf16[544,256]{1,0:T(8,128)(2,1)S(1)}, bf16[544,256]{1,0:T(8,128)(2,1)S(1)}, u32[]{:S(2)}, u32[]{:S(2)}) collective-permute-start(bf16[544,256]{1,0:T(8,128)(2,1)S(1)} %get-tuple-element.49.refs_0_), channel_id=1, source_target_pairs={{0,1},{1,0},{2,3},{3,2},{4,5},{5,4},{6,7},{7,6},{8,9},{9,8},{10,11... | collective-permute-start | bytes 835592 | tf_op jit(solution)/shard_map/ppermute | solution.py:313
  15.2 10.8 %collective-permute-start.4 = (bf16[544,256]{1,0:T(8,128)(2,1)S(1)}, bf16[544,256]{1,0:T(8,128)(2,1)S(1)}, u32[]{:S(2)}, u32[]{:S(2)}) collective-permute-start(bf16[544,256]{1,0:T(8,128)(2,1)S(1)} %collective-permute-done.refs_1_), channel_id=1, source_target_pairs={{0,1},{1,0},{2,3},{3,2},{4,5},{5,4},{6,7},{7,6},{8,9},{9,8},{10,11... | collective-permute-start | bytes 835592 | tf_op jit(solution)/shard_map/ppermute | solution.py:313
  21.8 4.2 %collective-permute-start.5 = (bf16[544,256]{1,0:T(8,128)(2,1)S(1)}, bf16[544,256]{1,0:T(8,128)(2,1)S(1)}, u32[]{:S(2)}, u32[]{:S(2)}) collective-permute-start(bf16[544,256]{1,0:T(8,128)(2,1)S(1)} %collective-permute-done.1.refs_2_), channel_id=1, source_target_pairs={{0,1},{1,0},{2,3},{3,2},{4,5},{5,4},{6,7},{7,6},{8,9},{9,8},{10,11... | collective-permute-start | bytes 835592 | tf_op jit(solution)/shard_map/ppermute | solution.py:313
  22.3 3.7 %collective-permute-start.6 = (bf16[544,256]{1,0:T(8,128)(2,1)S(1)}, bf16[544,256]{1,0:T(8,128)(2,1)S(1)}, u32[]{:S(2)}, u32[]{:S(2)}) collective-permute-start(bf16[544,256]{1,0:T(8,128)(2,1)S(1)} %collective-permute-done.2.refs_3_), channel_id=1, source_target_pairs={{0,1},{1,0},{2,3},{3,2},{4,5},{5,4},{6,7},{7,6},{8,9},{9,8},{10,11... | collective-permute-start | bytes 835592 | tf_op jit(solution)/shard_map/ppermute | solution.py:313
  34.9 23.0 %all-to-all-start = ((bf16[16,96,256]{2,1,0:T(8,128)(2,1)}), bf16[16,96,256]{2,1,0:T(8,128)(2,1)S(1)}, u32[]{:S(2)}, u32[]{:S(2)}) async-start(bf16[16,96,256]{2,1,0:T(8,128)(2,1)} %bitcast.40), calls=%async_computation | async-start | bytes 1572864 | tf_op jit(solution)/shard_map/all_to_all | solution.py:317
  42.4 9.2 %collective-permute-start.7 = (bf16[512,256]{1,0:T(8,128)(2,1)S(1)}, bf16[512,256]{1,0:T(8,128)(2,1)S(1)}, u32[]{:S(2)}, u32[]{:S(2)}) collective-permute-start(bf16[512,256]{1,0:T(8,128)(2,1)S(1)} %get-tuple-element.55), channel_id=1, source_target_pairs={{0,64},{32,96},{64,0},{96,32},{1,65},{33,97},{65,1},{97,33},{2,66}... | collective-permute-start | bytes 786440 | tf_op jit(solution)/shard_map/ppermute | solution.py:309
  44.3 13.5 %collective-permute-start.8 = (bf16[512,256]{1,0:T(8,128)(2,1)S(1)}, bf16[512,256]{1,0:T(8,128)(2,1)S(1)}, u32[]{:S(2)}, u32[]{:S(2)}) collective-permute-start(bf16[512,256]{1,0:T(8,128)(2,1)S(1)} %get-tuple-element.56), channel_id=1, source_target_pairs={{0,32},{32,64},{64,96},{96,0},{1,33},{33,65},{65,97},{97,1},{2,34}... | collective-permute-start | bytes 786440 | tf_op jit(solution)/shard_map/ppermute | solution.py:309
  45.4 12.5 %collective-permute-start.9 = (bf16[512,256]{1,0:T(8,128)(2,1)S(1)}, bf16[512,256]{1,0:T(8,128)(2,1)S(1)}, u32[]{:S(2)}, u32[]{:S(2)}) collective-permute-start(bf16[512,256]{1,0:T(8,128)(2,1)S(1)} %get-tuple-element.57), channel_id=1, source_target_pairs={{0,96},{32,0},{64,32},{96,64},{1,97},{33,1},{65,33},{97,65},{2,98}... | collective-permute-start | bytes 786440 | tf_op jit(solution)/shard_map/ppermute | solution.py:309
  59.0 20.0 %all-to-all-start.1 = ((bf16[16,96,256]{2,1,0:T(8,128)(2,1)}), bf16[16,96,256]{2,1,0:T(8,128)(2,1)S(1)}, u32[]{:S(2)}, u32[]{:S(2)}) async-start(bf16[16,96,256]{2,1,0:T(8,128)(2,1)} %get-tuple-element.63), calls=%async_computation.1 | async-start | bytes 1572864 | tf_op jit(solution)/shard_map/all_to_all | solution.py:317
  88.1 16.3 %all-to-all-start.2 = ((bf16[16,96,256]{2,1,0:T(8,128)(2,1)}), bf16[16,96,256]{2,1,0:T(8,128)(2,1)S(1)}, u32[]{:S(2)}, u32[]{:S(2)}) async-start(bf16[16,96,256]{2,1,0:T(8,128)(2,1)} %bitcast.42), calls=%async_computation.2 | async-start | bytes 1572864 | tf_op jit(solution)/shard_map/all_to_all | solution.py:317
  91.9 5.6 %collective-permute-start.14 = (bf16[256,256]{1,0:T(8,128)(2,1)}, bf16[256,256]{1,0:T(8,128)(2,1)S(1)}, u32[]{:S(2)}, u32[]{:S(2)}) collective-permute-start(bf16[256,256]{1,0:T(8,128)(2,1)} %get-tuple-element.71), channel_id=1, source_target_pairs={{0,64},{32,96},{64,0},{96,32},{1,65},{33,97},{65,1},{97,33},{2,66}... | collective-permute-start | bytes 393224 | tf_op jit(solution)/shard_map/ppermute | solution.py:309
  93.5 6.0 %collective-permute-start.15 = (bf16[256,256]{1,0:T(8,128)(2,1)}, bf16[256,256]{1,0:T(8,128)(2,1)S(1)}, u32[]{:S(2)}, u32[]{:S(2)}) collective-permute-start(bf16[256,256]{1,0:T(8,128)(2,1)} %get-tuple-element.72), channel_id=1, source_target_pairs={{0,96},{32,0},{64,32},{96,64},{1,97},{33,1},{65,33},{97,65},{2,98}... | collective-permute-start | bytes 393224 | tf_op jit(solution)/shard_map/ppermute | solution.py:309
  95.2 6.7 %collective-permute-start.16 = (bf16[256,256]{1,0:T(8,128)(2,1)}, bf16[256,256]{1,0:T(8,128)(2,1)S(1)}, u32[]{:S(2)}, u32[]{:S(2)}) collective-permute-start(bf16[256,256]{1,0:T(8,128)(2,1)} %get-tuple-element.73), channel_id=1, source_target_pairs={{0,32},{32,64},{64,96},{96,0},{1,33},{33,65},{65,97},{97,1},{2,34}... | collective-permute-start | bytes 393224 | tf_op jit(solution)/shard_map/ppermute | solution.py:309
  105.6 15.8 %all-to-all-start.3 = ((bf16[16,96,256]{2,1,0:T(8,128)(2,1)}), bf16[16,96,256]{2,1,0:T(8,128)(2,1)S(1)}, u32[]{:S(2)}, u32[]{:S(2)}) async-start(bf16[16,96,256]{2,1,0:T(8,128)(2,1)} %get-tuple-element.76), calls=%async_computation.3 | async-start | bytes 1572864 | tf_op jit(solution)/shard_map/all_to_all | solution.py:317
  109.6 3.8 %collective-permute-start.17 = (bf16[256,256]{1,0:T(8,128)(2,1)S(1)}, bf16[256,256]{1,0:T(8,128)(2,1)S(1)}, u32[]{:S(2)}, u32[]{:S(2)}) collective-permute-start(bf16[256,256]{1,0:T(8,128)(2,1)S(1)} %copy-done.5), channel_id=1, source_target_pairs={{0,1},{1,0},{2,3},{3,2},{4,5},{5,4},{6,7},{7,6},{8,9},{9,8},{10,11... | collective-permute-start | bytes 393224 | tf_op jit(solution)/shard_map/ppermute | solution.py:313
  140.1 20.5 %all-to-all-start.4 = ((bf16[16,96,256]{2,1,0:T(8,128)(2,1)}), bf16[16,96,256]{2,1,0:T(8,128)(2,1)S(1)}, u32[]{:S(2)}, u32[]{:S(2)}) async-start(bf16[16,96,256]{2,1,0:T(8,128)(2,1)} %bitcast.38), calls=%async_computation.4 | async-start | bytes 1572864 | tf_op jit(solution)/shard_map/all_to_all | solution.py:317
  143.7 7.2 %collective-permute-start.22 = (bf16[544,256]{1,0:T(8,128)(2,1)}, bf16[544,256]{1,0:T(8,128)(2,1)S(1)}, u32[]{:S(2)}, u32[]{:S(2)}) collective-permute-start(bf16[544,256]{1,0:T(8,128)(2,1)} %get-tuple-element.87), channel_id=1, source_target_pairs={{0,64},{32,96},{64,0},{96,32},{1,65},{33,97},{65,1},{97,33},{2,66}... | collective-permute-start | bytes 835592 | tf_op jit(solution)/shard_map/ppermute | solution.py:309
  144.8 12.9 %collective-permute-start.23 = (bf16[544,256]{1,0:T(8,128)(2,1)}, bf16[544,256]{1,0:T(8,128)(2,1)S(1)}, u32[]{:S(2)}, u32[]{:S(2)}) collective-permute-start(bf16[544,256]{1,0:T(8,128)(2,1)} %get-tuple-element.88), channel_id=1, source_target_pairs={{0,96},{32,0},{64,32},{96,64},{1,97},{33,1},{65,33},{97,65},{2,98}... | collective-permute-start | bytes 835592 | tf_op jit(solution)/shard_map/ppermute | solution.py:309
  146.6 13.5 %collective-permute-start.24 = (bf16[544,256]{1,0:T(8,128)(2,1)}, bf16[544,256]{1,0:T(8,128)(2,1)S(1)}, u32[]{:S(2)}, u32[]{:S(2)}) collective-permute-start(bf16[544,256]{1,0:T(8,128)(2,1)} %get-tuple-element.89), channel_id=1, source_target_pairs={{0,32},{32,64},{64,96},{96,0},{1,33},{33,65},{65,97},{97,1},{2,34}... | collective-permute-start | bytes 835592 | tf_op jit(solution)/shard_map/ppermute | solution.py:309
  146.6 14.3 %collective-permute-start.25 = (bf16[544,256]{1,0:T(8,128)(2,1)}, bf16[544,256]{1,0:T(8,128)(2,1)S(1)}, u32[]{:S(2)}, u32[]{:S(2)}) collective-permute-start(bf16[544,256]{1,0:T(8,128)(2,1)} %get-tuple-element.86.refs_0_), channel_id=1, source_target_pairs={{0,1},{1,0},{2,3},{3,2},{4,5},{5,4},{6,7},{7,6},{8,9},{9,8},{10,11... | collective-permute-start | bytes 835592 | tf_op jit(solution)/shard_map/ppermute | solution.py:313
  151.0 9.9 %collective-permute-start.26 = (bf16[544,256]{1,0:T(8,128)(2,1)S(1)}, bf16[544,256]{1,0:T(8,128)(2,1)S(1)}, u32[]{:S(2)}, u32[]{:S(2)}) collective-permute-start(bf16[544,256]{1,0:T(8,128)(2,1)S(1)} %collective-permute-done.22.refs_1_), channel_id=1, source_target_pairs={{0,1},{1,0},{2,3},{3,2},{4,5},{5,4},{6,7},{7,6},{8,9},{9,8},{10,11... | collective-permute-start | bytes 835592 | tf_op jit(solution)/shard_map/ppermute | solution.py:313
  (35 other events, 270.8 us)
where the time goes:
time: 166 us; the launch traced here: 165 us
  starting transfers between devices  66.4 us (40%)
  waiting for transfers between devices  45.9 us (28%)
  Pallas kernels  40.6 us (24%)
  local copies, waits for them, and re-layouts  7.51 us (5%)
  other arithmetic  3.52 us (2%)
    all_to_all x5, starting transfers between devices, scatter(): return lax.all_to_all(message, 'p', 0, 0, tiled=True)  24.9 us
    ppermute x12, waiting for transfers between devices, along(): lax.ppermute(m, 'z', pair)  23.7 us
    ppermute x16, starting transfers between devices, across(): lax.ppermute(message, 'c', [(0, 1), (1, 0)])  23.5 us
    all_to_all x5, waiting for transfers between devices, scatter(): return lax.all_to_all(message, 'p', 0, 0, tiled=True)  18.4 us
    ppermute x12, starting transfers between devices, along(): lax.ppermute(m, 'z', pair)  17.9 us
    pallas_call x1, Pallas kernels, body(): call(functools.partial(second_kernel, rows), messages_of(2 * rows + PAD)...  17.8 us
    pallas_call x1, Pallas kernels, body(): call(functools.partial(outer_kernel, rows), messages_of(rows) + (part_sha...  8.05 us
    pallas_call x1, Pallas kernels, body(): call(functools.partial(inner_kernel, rows), (shape(act_dims, F32), part_s...  7.89 us
  transfers between devices with their start and end apart: 34, of which 21 were waited for; matrix products, arithmetic and copies ran while one was open for 2% of the time, Pallas kernels for 2%

commit v1 on v0

--- a/solution.py
+++ b/solution.py
@@ -11,6 +11,8 @@
 EPSILON = 1e-05
 PAD = 16
 STEPS = 2
+ROW_BLOCK = 16
+COLUMN_BLOCK = 256
 F32 = jnp.float32
 BF16 = jnp.bfloat16
 
@@ -131,32 +133,6 @@
         out_ref[:, index] = value.astype(BF16).reshape(owners, share, width)
 
 
-def inner_kernel(rows, *refs):
-    sources, (wh_ref, wl_ref, act_ref, out_ref, acc_ref, held_ref, sem_ref) = refs[:-7], refs[-7:]
-    messages = pieces(sources[: len(sources) // 2], sources[len(sources) // 2 :])
-    copies = []
-    for step, group in groups_of(messages):
-        put = functools.partial(add_to, acc_ref, out_ref, step)
-        k, v = rows_of(group, 0, rows), rows_of(group, rows, rows)
-        r = rate_row(group, rows)
-        a = mm(wh_ref[0], k, (1, 1)) + mm(wl_ref[0], k, (1, 1))
-        b = mm(wh_ref[1], k, (1, 1)) + mm(wl_ref[1], k, (1, 1))
-        d = mm(wh_ref[2], v, (1, 1)) + mm(wl_ref[2], v, (1, 1))
-        held_ref[step, 0], held_ref[step, 1], held_ref[step, 2] = a, b, d
-        copies += start_all([(held_ref.at[step], act_ref.at[step])], sem_ref, step)
-        s = jax.nn.sigmoid(a)
-        sa = a * s
-        dh = d * r
-        hid_h, hid_l = halves(sa * b * r)
-        put(2, mm(hid_h, v) + mm(hid_l, v))
-        du_h, du_l = halves(dh * sa)
-        put(1, mm(du_h, k) + mm(du_l, k))
-        dg_h, dg_l = halves(dh * b * (s * (1.0 + a * (1.0 - s))))
-        put(0, mm(dg_h, k) + mm(dg_l, k))
-    for copy in copies:
-        copy.wait()
-
-
 def whole(ref, index):
     part = ref[:, index]
     return part.reshape(part.shape[0] * part.shape[1], part.shape[2])
@@ -168,85 +144,150 @@
         ref[start : start + rows] = rounded[slot * rows : (slot + 1) * rows]
 
 
+def put_halves(x_ref, high, low, at, value):
+    x_ref[(high, *at)], x_ref[(low, *at)] = halves(value)
+
+
+def by_blocks(hid, tokens, visit):
+    totals = [None] * (tokens // COLUMN_BLOCK)
+    for start in range(0, hid, ROW_BLOCK):
+        rows = slice(start, start + ROW_BLOCK)
+        for column in range(tokens // COLUMN_BLOCK):
+            columns = slice(column * COLUMN_BLOCK, (column + 1) * COLUMN_BLOCK)
+            found = visit((rows, columns), columns)
+            totals[column] = found if totals[column] is None or found is None else totals[column] + found
+    return totals
+
+
+def forward_halves(p_ref, x_ref, r):
+    def visit(at, columns):
+        a, b, d = p_ref[(0, *at)], p_ref[(1, *at)], p_ref[(2, *at)]
+        s = jax.nn.sigmoid(a)
+        sa = a * s
+        hid = sa * b
+        if r is not None:
+            hid, d = hid * r[:, columns], d * r[:, columns]
+        put_halves(x_ref, 4, 5, at, hid)
+        put_halves(x_ref, 2, 3, at, d * sa)
+        put_halves(x_ref, 0, 1, at, d * b * (s * (1.0 + a * (1.0 - s))))
+
+    by_blocks(p_ref.shape[1], p_ref.shape[2], visit)
+
+
+def first_products(p_ref, wh_ref, wl_ref, k, v):
+    for index, operand in enumerate((k, k, v)):
+        p_ref[index] = mm(wh_ref[index], operand, (1, 1)) + mm(wl_ref[index], operand, (1, 1))
+
+
+def inner_kernel(rows, *refs):
+    sources, (wh_ref, wl_ref, out_ref, acc_ref, p_ref, x_ref) = refs[:-6], refs[-6:]
+    messages = pieces(sources[: len(sources) // 2], sources[len(sources) // 2 :])
+    for step, group in groups_of(messages):
+        put = functools.partial(add_to, acc_ref, out_ref, step)
+        k, v = rows_of(group, 0, rows), rows_of(group, rows, rows)
+        first_products(p_ref, wh_ref, wl_ref, k, v)
+        forward_halves(p_ref, x_ref, rate_row(group, rows))
+        for index, operand in enumerate((k, k, v)):
+            put(index, mm(x_ref[2 * index], operand) + mm(x_ref[2 * index + 1], operand))
+
+
 def outer_kernel(rows, *refs):
-    layers = (len(refs) - 5) // 3
+    layers = (len(refs) - 8) // 3
     messages, n_ref = pieces(refs[:layers], refs[layers : 2 * layers]), refs[2 * layers]
-    gifts, (out_ref, acc_ref, held_ref, sem_ref) = refs[2 * layers + 1 : -4], refs[-4:]
+    gifts, rest = refs[2 * layers + 1 : -7], refs[-7:]
+    out_ref, acc_ref, held_ref, p_ref, x_ref, left_ref, sem_ref = rest
     gifts = pieces(gifts, gifts)
     copies = []
-    gate, up, down = whole(n_ref, 0), whole(n_ref, 1), whole(n_ref, 2)
+    hid = acc_ref.shape[1]
+    parts = [whole(n_ref, index) for index in range(3)]
+    for index in range(4):
+        left_ref[:, index * hid : (index + 1) * hid] = parts[index // 2].T
     for (step, group), (_, back) in zip(groups_of(messages), groups_of(gifts)):
         put = functools.partial(add_to, acc_ref, out_ref, step)
         q, g = rows_of(group, 0, rows), rows_of(group, rows, rows)
-        a, b, d = mm(gate, q, (1, 1)), mm(up, q, (1, 1)), mm(down, g, (1, 1))
+        for index, operand in enumerate((q, q, g)):
+            p_ref[index] = mm(parts[index], operand, (1, 1))
+        forward_halves(p_ref, x_ref, None)
+        stacked = x_ref[0:4].reshape(4 * hid, x_ref.shape[2])
+        held = [held_ref.at[step * len(back) + slot] for slot in range(len(back))]
+        give(held, mm(left_ref[...], stacked), 0, rows)
+        copies += start_all(list(zip(held, back)), sem_ref, step * len(back))
+        for index, operand in enumerate((q, q, g)):
+            put(index, mm(x_ref[2 * index], operand) + mm(x_ref[2 * index + 1], operand))
+    for copy in copies:
+        copy.wait()
+
+
+def second_halves(act_ref, p_ref, x_ref, r):
+    def visit(at, columns):
+        a, b, d = act_ref[(0, *at)], act_ref[(1, *at)], act_ref[(2, *at)]
+        big_a, big_b, e = p_ref[(0, *at)], p_ref[(1, *at)], p_ref[(2, *at)]
+        rate = r[:, columns]
         s = jax.nn.sigmoid(a)
         sa = a * s
-        hid_h, hid_l = halves(sa * b)
-        put(2, mm(hid_h, g) + mm(hid_l, g))
-        du_h, du_l = halves(d * sa)
-        put(1, mm(du_h, q) + mm(du_l, q))
-        dg_h, dg_l = halves(d * b * (s * (1.0 + a * (1.0 - s))))
-        put(0, mm(dg_h, q) + mm(dg_l, q))
-        dq = mm(gate, dg_h, (0, 0)) + mm(gate, dg_l, (0, 0))
-        dq += mm(up, du_h, (0, 0)) + mm(up, du_l, (0, 0))
-        held = [held_ref.at[step * len(back) + slot] for slot in range(len(back))]
-        give(held, dq, 0, rows)
-        copies += start_all(list(zip(held, back)), sem_ref, step * len(back))
-    for copy in copies:
-        copy.wait()
+        left = 1.0 - s
+        ds = s * (1.0 + a * left)
+        dds = s * left * (2.0 + a * (left - s))
+        dh, er = d * rate, e * rate
+        bds, dhds = b * ds, dh * ds
+        hid = sa * b
+        ddh = big_a * bds + big_b * sa
+        put_halves(x_ref, 0, 1, at, dh * bds)
+        put_halves(x_ref, 2, 3, at, dh * sa)
+        put_halves(x_ref, 6, 4, at, er * bds + big_b * dhds + big_a * (dh * b * dds))
+        put_halves(x_ref, 7, 5, at, er * sa + big_a * dhds)
+        put_halves(x_ref, 8, 9, at, hid * rate)
+        put_halves(x_ref, 11, 10, at, ddh * rate)
+        return hid * e + ddh * d
+
+    totals = by_blocks(p_ref.shape[1], p_ref.shape[2], visit)
+    return jnp.concatenate([jnp.sum(t, axis=0, keepdims=True) for t in totals], axis=1)
 
 
 def second_kernel(rows, *refs):
-    layers = (len(refs) - 12) // 3
+    layers = (len(refs) - 14) // 3
     sources = pieces(refs[:layers], refs[layers : 2 * layers])
-    wh_ref, wl_ref, c_ref, stored_ref = refs[2 * layers : 2 * layers + 4]
-    gifts, rest = refs[2 * layers + 4 : -8], refs[-8:]
+    wh_ref, wl_ref, c_ref = refs[2 * layers : 2 * layers + 3]
+    gifts, rest = refs[2 * layers + 3 : -11], refs[-11:]
     gifts = pieces(gifts, gifts)
-    out_ref, acc_ref, message_ref, act_ref, held_ref, message_sem, act_sem, held_sem = rest
+    out_ref, acc_ref, message_ref, act_ref, held_ref, p_ref, x_ref = rest[:7]
+    key_left, value_left, message_sem, held_sem = rest[7:]
     messages = [message_ref.at[slot] for slot in range(len(sources))]
     loads = start_all(list(zip(sources, messages)), message_sem)
-    act_loads = start_all([(stored_ref.at[step], act_ref.at[step]) for step in range(STEPS)], act_sem)
     copies = []
-    gate, up, down = whole(c_ref, 0), whole(c_ref, 1), whole(c_ref, 2)
+    hid = acc_ref.shape[1]
+    parts = [whole(c_ref, index) for index in range(3)]
+    gate, up, down = [part.T for part in parts]
+    high, low = [wh_ref[index].T for index in range(3)], [wl_ref[index].T for index in range(3)]
+    for left_ref, items in (
+        (key_left, (gate, gate, up, up, high[0], high[1], high[0], high[1], low[0], low[1])),
+        (value_left, (down, down, high[2], high[2], low[2])),
+    ):
+        for index, item in enumerate(items):
+            left_ref[:, index * hid : (index + 1) * hid] = item
     for (step, group), (_, back) in zip(groups_of(messages), groups_of(gifts)):
         put = functools.partial(add_to, acc_ref, out_ref, step)
         for load in loads[step * len(group) : (step + 1) * len(group)]:
             load.wait()
         k, v = rows_of(group, 0, rows), rows_of(group, rows, rows)
-        r = rate_row(group, rows)
-        big_a, big_b, e = mm(gate, k, (1, 1)), mm(up, k, (1, 1)), mm(down, v, (1, 1))
-        act_loads[step].wait()
-        a, b, d = act_ref[step, 0], act_ref[step, 1], act_ref[step, 2]
-        s = jax.nn.sigmoid(a)
-        sa = a * s
-        ds = s * (1.0 + a * (1.0 - s))
-        dds = s * (1.0 - s) * (2.0 + a * (1.0 - 2.0 * s))
-        dh, er = d * r, e * r
-        bds = b * ds
-        hid = sa * b
-        ddh = big_a * bds + big_b * sa
-        d_rate = jnp.sum(hid * e + ddh * d, axis=0, keepdims=True)
-        db_h, db_l = halves(er * sa + big_a * (dh * ds))
-        da_h, da_l = halves((er * b + big_b * dh) * ds + big_a * (dh * b * dds))
-        put(0, mm(da_h, k) + mm(da_l, k))
-        put(1, mm(db_h, k) + mm(db_l, k))
-        dr_h, dr_l = halves(ddh * r)
-        put(2, mm(dr_h, v) + mm(dr_l, v))
-        hid_h, hid_l = halves(hid * r)
-        dv = mm(down, hid_h, (0, 0)) + mm(down, hid_l, (0, 0))
-        dv += mm(wh_ref[2], dr_h, (0, 0)) + mm(wh_ref[2], dr_l, (0, 0)) + mm(wl_ref[2], dr_h, (0, 0))
-        dg_h, dg_l = halves(dh * bds)
-        du_h, du_l = halves(dh * sa)
-        dk = mm(gate, dg_h, (0, 0)) + mm(gate, dg_l, (0, 0))
-        dk += mm(up, du_h, (0, 0)) + mm(up, du_l, (0, 0))
-        dk += mm(wh_ref[0], da_h, (0, 0)) + mm(wh_ref[0], da_l, (0, 0)) + mm(wl_ref[0], da_h, (0, 0))
-        dk += mm(wh_ref[1], db_h, (0, 0)) + mm(wh_ref[1], db_l, (0, 0)) + mm(wl_ref[1], db_h, (0, 0))
+        for index, operand in enumerate((k, k, v)):
+            p_ref[index] = mm(parts[index], operand, (1, 1))
+        first_products(act_ref, wh_ref, wl_ref, k, v)
+        d_rate = second_halves(act_ref, p_ref, x_ref, rate_row(group, rows))
+
+        def stacked(first, last):
+            return x_ref[first:last].reshape((last - first) * hid, x_ref.shape[2])
+
+        dk = mm(key_left[:, : 8 * hid], stacked(0, 8)) + mm(key_left[:, 8 * hid :], stacked(6, 8))
+        dv = mm(value_left[:, : 4 * hid], stacked(8, 12)) + mm(value_left[:, 4 * hid :], x_ref[11])
         held = [held_ref.at[step * len(back) + slot] for slot in range(len(back))]
         give(held, dk, 0, rows)
         give(held, dv, rows, rows)
         for slot, ref in enumerate(held):
             ref[2 * rows :] = padded_row(d_rate[:, slot * rows : (slot + 1) * rows], ref.shape[1])
         copies += start_all(list(zip(held, back)), held_sem, step * len(back))
+        for index, (one, two, operand) in enumerate(((6, 4, k), (7, 5, k), (11, 10, v))):
+            put(index, mm(x_ref[one], operand) + mm(x_ref[two], operand))
     for copy in copies:
         copy.wait()
 
@@ -340,21 +381,23 @@
         1,
     )
     part_shape = shape((owners, 3, share, width), BF16)
-    act_dims = (STEPS, 3, hid, heads * rows // STEPS)
     scratch = [pltpu.VMEM((3, hid, width), F32)]
+    group_tokens = heads * rows // STEPS
+    products = pltpu.VMEM((3, hid, group_tokens), F32)
+    half_terms = pltpu.VMEM((6, hid, group_tokens), BF16)
     main = pl.BlockSpec(memory_space=pltpu.HBM)
-    acts, grad_part = call(
+    grad_part = call(
         functools.partial(inner_kernel, rows),
-        (shape(act_dims, F32), part_shape),
+        part_shape,
         flops=12 * product,
         vmem=60,
         in_specs=[memory] * (heads + 2),
-        out_specs=[main, memory],
-        scratch_shapes=scratch + [pltpu.VMEM(act_dims, F32), pltpu.SemaphoreType.DMA((STEPS,))],
+        out_specs=memory,
+        scratch_shapes=scratch + [products, half_terms],
     )(*kv, w_high, w_low)
     own_shape = shape((3 * share, width), F32)
     spread_shape = shape((owners, 3 * share, width), BF16)
-    summed, qg = lax.optimization_barrier((scatter(grad_part), qg))
+    summed, qg[1] = lax.optimization_barrier((scatter(grad_part), qg[1]))
     updated, moved = call(update_kernel, (spread_shape, own_shape))(summed, own)
     updated, got = lax.optimization_barrier((scatter(updated), across(qg)))
     updated, qg = updated.reshape(owners, 3, share, width), qg + got
@@ -366,7 +409,13 @@
         in_specs=[memory] * (heads + 1),
         out_specs=[main] * layers + [memory],
         scratch_shapes=scratch
-        + [pltpu.VMEM((heads, rows, width), BF16), pltpu.SemaphoreType.DMA((heads,))],
+        + [
+            pltpu.VMEM((heads, rows, width), BF16),
+            products,
+            half_terms,
+            pltpu.VMEM((width, 4 * hid), BF16),
+            pltpu.SemaphoreType.DMA((heads,)),
+        ],
     )(*qg, updated)
     given, d_queries = lax.optimization_barrier((scatter(d_part), along(d_queries, -1)))
     cotangent, direct = call(back_kernel, (spread_shape, own_shape))(given, own, moved)
@@ -382,18 +431,21 @@
         messages_of(2 * rows + PAD) + (part_shape,),
         flops=24 * product,
         vmem=60,
-        in_specs=[main] * heads + [memory] * 3 + [main],
+        in_specs=[main] * heads + [memory] * 3,
         out_specs=[main] * layers + [memory],
         scratch_shapes=scratch
         + [
             pltpu.VMEM((heads, 2 * rows + PAD, width), BF16),
-            pltpu.VMEM(act_dims, F32),
+            products,
             pltpu.VMEM((heads, 2 * rows + PAD, width), BF16),
+            products,
+            pltpu.VMEM((12, hid, group_tokens), BF16),
+            pltpu.VMEM((width, 10 * hid), BF16),
+            pltpu.VMEM((width, 5 * hid), BF16),
             pltpu.SemaphoreType.DMA((heads,)),
-            pltpu.SemaphoreType.DMA((STEPS,)),
             pltpu.SemaphoreType.DMA((heads,)),
         ],
-    )(*kv, w_high, w_low, cotangent, acts)
+    )(*kv, w_high, w_low, cotangent)
     d_kv = along(d_kv, -1)
     key_grad, value_grad, step_grad = call(
         unpack_kv_kernel,

time: 166 us -> 160 us (0.964)
  Pallas kernels: 40.6 us -> 37 us
  waiting for transfers between devices: 45.9 us -> 42.9 us
    pallas_call x1, Pallas kernels: 17.8 us -> 15 us  [body(): call(functools.partial(second_kernel, rows), messages_of(2 * rows + PAD)...]
    all_to_all x5, waiting for transfers between devices: 18.4 us -> 16.5 us  [scatter(): return lax.all_to_all(message, 'p', 0, 0, tiled=True)]
  transfers between devices with their start and end apart: 34 -> 34, of which waited for: 21 -> 22; matrix products, arithmetic and copies ran while one was open for 2% -> 2% of each run, Pallas kernels for 2% -> 2%
where the time goes in v1:
time: 160 us; the launch traced here: 159 us
  starting transfers between devices  67.5 us (42%)
  waiting for transfers between devices  42.9 us (27%)
  Pallas kernels  37 us (23%)
  local copies, waits for them, and re-layouts  7.49 us (5%)
  other arithmetic  3.47 us (2%)
    ppermute x16, starting transfers between devices, across(): lax.ppermute(message, 'c', [(0, 1), (1, 0)])  24.4 us
    all_to_all x5, starting transfers between devices, scatter(): return lax.all_to_all(message, 'p', 0, 0, tiled=True)  23.7 us
    ppermute x12, waiting for transfers between devices, along(): lax.ppermute(m, 'z', pair)  22.8 us
    ppermute x12, starting transfers between devices, along(): lax.ppermute(m, 'z', pair)  18.8 us
    all_to_all x5, waiting for transfers between devices, scatter(): return lax.all_to_all(message, 'p', 0, 0, tiled=True)  16.5 us
    pallas_call x1, Pallas kernels, body(): call(functools.partial(second_kernel, rows), messages_of(2 * rows + PAD)...  15 us
    pallas_call x1, Pallas kernels, body(): call(functools.partial(outer_kernel, rows), messages_of(rows) + (part_sha...  7.92 us
    pallas_call x1, Pallas kernels, body(): call(functools.partial(inner_kernel, rows), part_shape, flops=12 * produc...  7.32 us
  transfers between devices with their start and end apart: 34, of which 22 were waited for; matrix products, arithmetic and copies ran while one was open for 2% of the time, Pallas kernels for 2%

profile of v1, /device:TPU:1, one launch (start us, length us, event | category | flops | bytes accessed | tf_op | source)
XLA Modules:
  0.0 159.4 jit_solution(6562390808398221242)
XLA Ops:
  4.2 4.5 %collective-permute-start = (bf16[544,256]{1,0:T(8,128)(2,1)S(1)}, bf16[544,256]{1,0:T(8,128)(2,1)S(1)}, u32[]{:S(2)}, u32[]{:S(2)}) collective-permute-start(bf16[544,256]{1,0:T(8,128)(2,1)S(1)} %get-tuple-element.45), channel_id=1, source_target_pairs={{0,64},{32,96},{64,0},{96,32},{1,65},{33,97},{65,1},{97,33},{2,66}... | collective-permute-start | bytes 835592 | tf_op jit(solution)/shard_map/ppermute | solution.py:350
  12.9 2.2 %collective-permute-done.refs_1_ = bf16[544,256]{1,0:T(8,128)(2,1)S(1)} collective-permute-done((bf16[544,256]{1,0:T(8,128)(2,1)S(1)}, bf16[544,256]{1,0:T(8,128)(2,1)S(1)}, u32[]{:S(2)}, u32[]{:S(2)}) %collective-permute-start) | collective-permute-done | bytes 278560 | tf_op jit(solution)/shard_map/ppermute | solution.py:350
  17.2 4.6 %collective-permute-done.1.refs_2_ = bf16[544,256]{1,0:T(8,128)(2,1)S(1)} collective-permute-done((bf16[544,256]{1,0:T(8,128)(2,1)S(1)}, bf16[544,256]{1,0:T(8,128)(2,1)S(1)}, u32[]{:S(2)}, u32[]{:S(2)}) %collective-permute-start.1) | collective-permute-done | bytes 278560 | tf_op jit(solution)/shard_map/ppermute | solution.py:350
  23.1 2.8 %fusion = (bf16[3,512,256]{2,1,0:T(8,128)(2,1)}, bf16[3,512,256]{2,1,0:T(8,128)(2,1)}) fusion(f32[2,3,512,256]{3,2,1,0:T(8,128)} %param.10, s32[]{:T(128)S(6)} %select_n.82), kind=kLoop, calls=%fused_computation.2 | loop fusion | flops 1572864 | bytes 3145732 | tf_op jit(solution)/shard_map/convert_element_type | solution.py:363
  27.0 7.3 %shard_map.103 = bf16[16,3,32,256]{3,2,1,0:T(8,128)(2,1)} custom-call(bf16[544,256]{1,0:T(8,128)(2,1)} %copy-done.7, bf16[544,256]{1,0:T(8,128)(2,1)} %copy-done.11, bf16[544,256]{1,0:T(8,128)(2,1)} %copy-done.12, bf16[544,256]{1,0:T(8,128)(2,1)} %copy-done.13, bf16[544,256]{1,0:T(8,128)(2,1)} %copy-done.14, bf16[544,256]{1,0:T(8,128)(2,1)} %copy-done.15, ...), custom_call_target="tpu_custom_call" | custom-call | flops 3221225472 | bytes 4194304 | tf_op jit(solution)/shard_map/pallas_call | solution.py:389
  34.3 6.7 %all-to-all-start = ((bf16[16,96,256]{2,1,0:T(8,128)(2,1)}), bf16[16,96,256]{2,1,0:T(8,128)(2,1)S(1)}, u32[]{:S(2)}, u32[]{:S(2)}) async-start(bf16[16,96,256]{2,1,0:T(8,128)(2,1)} %bitcast.41), calls=%async_computation | async-start | bytes 1572864 | tf_op jit(solution)/shard_map/all_to_all | solution.py:358
  44.7 6.2 %collective-permute-done.7.refs_1_ = bf16[512,256]{1,0:T(8,128)(2,1)S(1)} collective-permute-done((bf16[512,256]{1,0:T(8,128)(2,1)S(1)}, bf16[512,256]{1,0:T(8,128)(2,1)S(1)}, u32[]{:S(2)}, u32[]{:S(2)}) %collective-permute-start.7) | collective-permute-done | bytes 262176 | tf_op jit(solution)/shard_map/ppermute | solution.py:350
  50.8 4.0 %all-to-all-done.in_ref = bf16[16,96,256]{2,1,0:T(8,128)(2,1)S(1)} async-done(((bf16[16,96,256]{2,1,0:T(8,128)(2,1)}), bf16[16,96,256]{2,1,0:T(8,128)(2,1)S(1)}, u32[]{:S(2)}, u32[]{:S(2)}) %all-to-all-start) | async-done | bytes 786464 | tf_op jit(solution)/shard_map/all_to_all | solution.py:358
  55.9 3.7 %all-to-all-start.1 = ((bf16[16,96,256]{2,1,0:T(8,128)(2,1)}), bf16[16,96,256]{2,1,0:T(8,128)(2,1)S(1)}, u32[]{:S(2)}, u32[]{:S(2)}) async-start(bf16[16,96,256]{2,1,0:T(8,128)(2,1)} %get-tuple-element.54), calls=%async_computation.1 | async-start | bytes 1572864 | tf_op jit(solution)/shard_map/all_to_all | solution.py:358
  60.3 2.1 %collective-permute-start.9 = (bf16[512,256]{1,0:T(8,128)(2,1)S(1)}, bf16[512,256]{1,0:T(8,128)(2,1)S(1)}, u32[]{:S(2)}, u32[]{:S(2)}) collective-permute-start(bf16[512,256]{1,0:T(8,128)(2,1)S(1)} %get-tuple-element.52), channel_id=1, source_target_pairs={{0,96},{32,0},{64,32},{96,64},{1,97},{33,1},{65,33},{97,65},{2,98}... | collective-permute-start | bytes 786440 | tf_op jit(solution)/shard_map/ppermute | solution.py:350
  64.4 2.8 %collective-permute-done.8.refs_2_ = bf16[512,256]{1,0:T(8,128)(2,1)S(1)} collective-permute-done((bf16[512,256]{1,0:T(8,128)(2,1)S(1)}, bf16[512,256]{1,0:T(8,128)(2,1)S(1)}, u32[]{:S(2)}, u32[]{:S(2)}) %collective-permute-start.8) | collective-permute-done | bytes 262176 | tf_op jit(solution)/shard_map/ppermute | solution.py:350
  67.3 2.4 %collective-permute-start.12 = (bf16[512,256]{1,0:T(8,128)(2,1)S(1)}, bf16[512,256]{1,0:T(8,128)(2,1)S(1)}, u32[]{:S(2)}, u32[]{:S(2)}) collective-permute-start(bf16[512,256]{1,0:T(8,128)(2,1)S(1)} %collective-permute-done.8.refs_2_), channel_id=1, source_target_pairs={{0,1},{1,0},{2,3},{3,2},{4,5},{5,4},{6,7},{7,6},{8,9},{9,8},{10,11... | collective-permute-start | bytes 786440 | tf_op jit(solution)/shard_map/ppermute | solution.py:354
  73.3 7.9 %shard_map.105 = (bf16[256,256]{1,0:T(8,128)(2,1)}, bf16[256,256]{1,0:T(8,128)(2,1)}, bf16[256,256]{1,0:T(8,128)(2,1)}, bf16[256,256]{1,0:T(8,128)(2,1)}, bf16[16,3,32,256]{3,2,1,0:T(8,128)(2,1)}) custom-call(bf16[512,256]{1,0:T(8,128)(2,1)} %copy-done.8, bf16[512,256]{1,0:T(8,128)(2,1)} %copy-done.18, bf16[512,256]{1,0:T(8,128)(2,1)} %copy-done.19, ...), custom_call_target="tpu_custom_call" | custom-call | flops 3489660928 | bytes 4194304 | tf_op jit(solution)/shard_map/pallas_call | solution.py:404
  81.2 6.0 %all-to-all-start.2 = ((bf16[16,96,256]{2,1,0:T(8,128)(2,1)}), bf16[16,96,256]{2,1,0:T(8,128)(2,1)S(1)}, u32[]{:S(2)}, u32[]{:S(2)}) async-start(bf16[16,96,256]{2,1,0:T(8,128)(2,1)} %bitcast.42), calls=%async_computation.2 | async-start | bytes 1572864 | tf_op jit(solution)/shard_map/all_to_all | solution.py:358
  90.7 2.7 %collective-permute-done.14.refs_1_ = bf16[256,256]{1,0:T(8,128)(2,1)S(1)} collective-permute-done((bf16[256,256]{1,0:T(8,128)(2,1)}, bf16[256,256]{1,0:T(8,128)(2,1)S(1)}, u32[]{:S(2)}, u32[]{:S(2)}) %collective-permute-start.14) | collective-permute-done | bytes 131104 | tf_op jit(solution)/shard_map/ppermute | solution.py:350
  93.4 2.8 %collective-permute-done.15.refs_2_ = bf16[256,256]{1,0:T(8,128)(2,1)S(1)} collective-permute-done((bf16[256,256]{1,0:T(8,128)(2,1)}, bf16[256,256]{1,0:T(8,128)(2,1)S(1)}, u32[]{:S(2)}, u32[]{:S(2)}) %collective-permute-start.15) | collective-permute-done | bytes 131104 | tf_op jit(solution)/shard_map/ppermute | solution.py:350
  96.6 4.2 %all-to-all-done.2.in_ref = bf16[16,96,256]{2,1,0:T(8,128)(2,1)S(1)} async-done(((bf16[16,96,256]{2,1,0:T(8,128)(2,1)}), bf16[16,96,256]{2,1,0:T(8,128)(2,1)S(1)}, u32[]{:S(2)}, u32[]{:S(2)}) %all-to-all-start.2) | async-done | bytes 786464 | tf_op jit(solution)/shard_map/all_to_all | solution.py:358
  101.9 3.6 %all-to-all-start.3 = ((bf16[16,96,256]{2,1,0:T(8,128)(2,1)}), bf16[16,96,256]{2,1,0:T(8,128)(2,1)S(1)}, u32[]{:S(2)}, u32[]{:S(2)}) async-start(bf16[16,96,256]{2,1,0:T(8,128)(2,1)} %get-tuple-element.67), calls=%async_computation.3 | async-start | bytes 1572864 | tf_op jit(solution)/shard_map/all_to_all | solution.py:358
  110.6 7.6 %all-to-all-done.3 = bf16[16,96,256]{2,1,0:T(8,128)(2,1)S(1)} async-done(((bf16[16,96,256]{2,1,0:T(8,128)(2,1)}), bf16[16,96,256]{2,1,0:T(8,128)(2,1)S(1)}, u32[]{:S(2)}, u32[]{:S(2)}) %all-to-all-start.3) | async-done | bytes 786464 | tf_op jit(solution)/shard_map/all_to_all | solution.py:358
  119.1 15.0 %shard_map.108 = (bf16[544,256]{1,0:T(8,128)(2,1)}, bf16[544,256]{1,0:T(8,128)(2,1)}, bf16[544,256]{1,0:T(8,128)(2,1)}, bf16[544,256]{1,0:T(8,128)(2,1)}, bf16[16,3,32,256]{3,2,1,0:T(8,128)(2,1)}) custom-call(bf16[544,256]{1,0:T(8,128)(2,1)} %copy-done.7, bf16[544,256]{1,0:T(8,128)(2,1)} %copy-done.11, bf16[544,256]{1,0:T(8,128)(2,1)} %copy-done.12, ...), custom_call_target="tpu_custom_call" | custom-call | flops 6442450944 | bytes 4194304 | tf_op jit(solution)/shard_map/pallas_call | solution.py:429
  134.1 3.6 %all-to-all-start.4 = ((bf16[16,96,256]{2,1,0:T(8,128)(2,1)}), bf16[16,96,256]{2,1,0:T(8,128)(2,1)S(1)}, u32[]{:S(2)}, u32[]{:S(2)}) async-start(bf16[16,96,256]{2,1,0:T(8,128)(2,1)} %bitcast.38), calls=%async_computation.4 | async-start | bytes 1572864 | tf_op jit(solution)/shard_map/all_to_all | solution.py:358
  141.2 3.5 %collective-permute-start.25 = (bf16[544,256]{1,0:T(8,128)(2,1)}, bf16[544,256]{1,0:T(8,128)(2,1)S(1)}, u32[]{:S(2)}, u32[]{:S(2)}) collective-permute-start(bf16[544,256]{1,0:T(8,128)(2,1)} %get-tuple-element.76.refs_0_), channel_id=1, source_target_pairs={{0,1},{1,0},{2,3},{3,2},{4,5},{5,4},{6,7},{7,6},{8,9},{9,8},{10,11... | collective-permute-start | bytes 835592 | tf_op jit(solution)/shard_map/ppermute | solution.py:354
  145.0 6.6 %collective-permute-start.26 = (bf16[544,256]{1,0:T(8,128)(2,1)S(1)}, bf16[544,256]{1,0:T(8,128)(2,1)S(1)}, u32[]{:S(2)}, u32[]{:S(2)}) collective-permute-start(bf16[544,256]{1,0:T(8,128)(2,1)S(1)} %collective-permute-done.22.refs_1_), channel_id=1, source_target_pairs={{0,1},{1,0},{2,3},{3,2},{4,5},{5,4},{6,7},{7,6},{8,9},{9,8},{10,11... | collective-permute-start | bytes 835592 | tf_op jit(solution)/shard_map/ppermute | solution.py:354
  152.4 2.1 %collective-permute-start.27 = (bf16[544,256]{1,0:T(8,128)(2,1)S(1)}, bf16[544,256]{1,0:T(8,128)(2,1)S(1)}, u32[]{:S(2)}, u32[]{:S(2)}) collective-permute-start(bf16[544,256]{1,0:T(8,128)(2,1)S(1)} %collective-permute-done.23.refs_2_), channel_id=1, source_target_pairs={{0,1},{1,0},{2,3},{3,2},{4,5},{5,4},{6,7},{7,6},{8,9},{9,8},{10,11... | collective-permute-start | bytes 835592 | tf_op jit(solution)/shard_map/ppermute | solution.py:354
  (110 shorter events, 43.4 us)
Async XLA Ops:
  4.2 10.9 %collective-permute-start = (bf16[544,256]{1,0:T(8,128)(2,1)S(1)}, bf16[544,256]{1,0:T(8,128)(2,1)S(1)}, u32[]{:S(2)}, u32[]{:S(2)}) collective-permute-start(bf16[544,256]{1,0:T(8,128)(2,1)S(1)} %get-tuple-element.45), channel_id=1, source_target_pairs={{0,64},{32,96},{64,0},{96,32},{1,65},{33,97},{65,1},{97,33},{2,66}... | collective-permute-start | bytes 835592 | tf_op jit(solution)/shard_map/ppermute | solution.py:350
  8.8 13.1 %collective-permute-start.1 = (bf16[544,256]{1,0:T(8,128)(2,1)S(1)}, bf16[544,256]{1,0:T(8,128)(2,1)S(1)}, u32[]{:S(2)}, u32[]{:S(2)}) collective-permute-start(bf16[544,256]{1,0:T(8,128)(2,1)S(1)} %get-tuple-element.46), channel_id=1, source_target_pairs={{0,32},{32,64},{64,96},{96,0},{1,33},{33,65},{65,97},{97,1},{2,34}... | collective-permute-start | bytes 835592 | tf_op jit(solution)/shard_map/ppermute | solution.py:350
  9.5 12.8 %collective-permute-start.2 = (bf16[544,256]{1,0:T(8,128)(2,1)S(1)}, bf16[544,256]{1,0:T(8,128)(2,1)S(1)}, u32[]{:S(2)}, u32[]{:S(2)}) collective-permute-start(bf16[544,256]{1,0:T(8,128)(2,1)S(1)} %get-tuple-element.47), channel_id=1, source_target_pairs={{0,96},{32,0},{64,32},{96,64},{1,97},{33,1},{65,33},{97,65},{2,98}... | collective-permute-start | bytes 835592 | tf_op jit(solution)/shard_map/ppermute | solution.py:350
  11.4 14.5 %collective-permute-start.3 = (bf16[544,256]{1,0:T(8,128)(2,1)S(1)}, bf16[544,256]{1,0:T(8,128)(2,1)S(1)}, u32[]{:S(2)}, u32[]{:S(2)}) collective-permute-start(bf16[544,256]{1,0:T(8,128)(2,1)S(1)} %get-tuple-element.44.refs_0_), channel_id=1, source_target_pairs={{0,1},{1,0},{2,3},{3,2},{4,5},{5,4},{6,7},{7,6},{8,9},{9,8},{10,11... | collective-permute-start | bytes 835592 | tf_op jit(solution)/shard_map/ppermute | solution.py:354
  15.2 10.8 %collective-permute-start.4 = (bf16[544,256]{1,0:T(8,128)(2,1)S(1)}, bf16[544,256]{1,0:T(8,128)(2,1)S(1)}, u32[]{:S(2)}, u32[]{:S(2)}) collective-permute-start(bf16[544,256]{1,0:T(8,128)(2,1)S(1)} %collective-permute-done.refs_1_), channel_id=1, source_target_pairs={{0,1},{1,0},{2,3},{3,2},{4,5},{5,4},{6,7},{7,6},{8,9},{9,8},{10,11... | collective-permute-start | bytes 835592 | tf_op jit(solution)/shard_map/ppermute | solution.py:354
  21.8 4.1 %collective-permute-start.5 = (bf16[544,256]{1,0:T(8,128)(2,1)S(1)}, bf16[544,256]{1,0:T(8,128)(2,1)S(1)}, u32[]{:S(2)}, u32[]{:S(2)}) collective-permute-start(bf16[544,256]{1,0:T(8,128)(2,1)S(1)} %collective-permute-done.1.refs_2_), channel_id=1, source_target_pairs={{0,1},{1,0},{2,3},{3,2},{4,5},{5,4},{6,7},{7,6},{8,9},{9,8},{10,11... | collective-permute-start | bytes 835592 | tf_op jit(solution)/shard_map/ppermute | solution.py:354
  34.3 20.5 %all-to-all-start = ((bf16[16,96,256]{2,1,0:T(8,128)(2,1)}), bf16[16,96,256]{2,1,0:T(8,128)(2,1)S(1)}, u32[]{:S(2)}, u32[]{:S(2)}) async-start(bf16[16,96,256]{2,1,0:T(8,128)(2,1)} %bitcast.41), calls=%async_computation | async-start | bytes 1572864 | tf_op jit(solution)/shard_map/all_to_all | solution.py:358
  41.8 9.0 %collective-permute-start.7 = (bf16[512,256]{1,0:T(8,128)(2,1)S(1)}, bf16[512,256]{1,0:T(8,128)(2,1)S(1)}, u32[]{:S(2)}, u32[]{:S(2)}) collective-permute-start(bf16[512,256]{1,0:T(8,128)(2,1)S(1)} %get-tuple-element.49), channel_id=1, source_target_pairs={{0,64},{32,96},{64,0},{96,32},{1,65},{33,97},{65,1},{97,33},{2,66}... | collective-permute-start | bytes 786440 | tf_op jit(solution)/shard_map/ppermute | solution.py:350
  55.9 16.4 %all-to-all-start.1 = ((bf16[16,96,256]{2,1,0:T(8,128)(2,1)}), bf16[16,96,256]{2,1,0:T(8,128)(2,1)S(1)}, u32[]{:S(2)}, u32[]{:S(2)}) async-start(bf16[16,96,256]{2,1,0:T(8,128)(2,1)} %get-tuple-element.54), calls=%async_computation.1 | async-start | bytes 1572864 | tf_op jit(solution)/shard_map/all_to_all | solution.py:358
  59.7 7.6 %collective-permute-start.8 = (bf16[512,256]{1,0:T(8,128)(2,1)S(1)}, bf16[512,256]{1,0:T(8,128)(2,1)S(1)}, u32[]{:S(2)}, u32[]{:S(2)}) collective-permute-start(bf16[512,256]{1,0:T(8,128)(2,1)S(1)} %get-tuple-element.51), channel_id=1, source_target_pairs={{0,32},{32,64},{64,96},{96,0},{1,33},{33,65},{65,97},{97,1},{2,34}... | collective-permute-start | bytes 786440 | tf_op jit(solution)/shard_map/ppermute | solution.py:350
  60.3 9.4 %collective-permute-start.9 = (bf16[512,256]{1,0:T(8,128)(2,1)S(1)}, bf16[512,256]{1,0:T(8,128)(2,1)S(1)}, u32[]{:S(2)}, u32[]{:S(2)}) collective-permute-start(bf16[512,256]{1,0:T(8,128)(2,1)S(1)} %get-tuple-element.52), channel_id=1, source_target_pairs={{0,96},{32,0},{64,32},{96,64},{1,97},{33,1},{65,33},{97,65},{2,98}... | collective-permute-start | bytes 786440 | tf_op jit(solution)/shard_map/ppermute | solution.py:350
  62.4 7.8 %collective-permute-start.10 = (bf16[512,256]{1,0:T(8,128)(2,1)S(1)}, bf16[512,256]{1,0:T(8,128)(2,1)S(1)}, u32[]{:S(2)}, u32[]{:S(2)}) collective-permute-start(bf16[512,256]{1,0:T(8,128)(2,1)S(1)} %get-tuple-element.48.refs_0_), channel_id=1, source_target_pairs={{0,1},{1,0},{2,3},{3,2},{4,5},{5,4},{6,7},{7,6},{8,9},{9,8},{10,11... | collective-permute-start | bytes 786440 | tf_op jit(solution)/shard_map/ppermute | solution.py:354
  81.2 19.5 %all-to-all-start.2 = ((bf16[16,96,256]{2,1,0:T(8,128)(2,1)}), bf16[16,96,256]{2,1,0:T(8,128)(2,1)S(1)}, u32[]{:S(2)}, u32[]{:S(2)}) async-start(bf16[16,96,256]{2,1,0:T(8,128)(2,1)} %bitcast.42), calls=%async_computation.2 | async-start | bytes 1572864 | tf_op jit(solution)/shard_map/all_to_all | solution.py:358
  87.2 6.2 %collective-permute-start.14 = (bf16[256,256]{1,0:T(8,128)(2,1)}, bf16[256,256]{1,0:T(8,128)(2,1)S(1)}, u32[]{:S(2)}, u32[]{:S(2)}) collective-permute-start(bf16[256,256]{1,0:T(8,128)(2,1)} %get-tuple-element.62), channel_id=1, source_target_pairs={{0,64},{32,96},{64,0},{96,32},{1,65},{33,97},{65,1},{97,33},{2,66}... | collective-permute-start | bytes 393224 | tf_op jit(solution)/shard_map/ppermute | solution.py:350
  89.3 7.0 %collective-permute-start.15 = (bf16[256,256]{1,0:T(8,128)(2,1)}, bf16[256,256]{1,0:T(8,128)(2,1)S(1)}, u32[]{:S(2)}, u32[]{:S(2)}) collective-permute-start(bf16[256,256]{1,0:T(8,128)(2,1)} %get-tuple-element.63), channel_id=1, source_target_pairs={{0,96},{32,0},{64,32},{96,64},{1,97},{33,1},{65,33},{97,65},{2,98}... | collective-permute-start | bytes 393224 | tf_op jit(solution)/shard_map/ppermute | solution.py:350
  89.9 6.7 %collective-permute-start.16 = (bf16[256,256]{1,0:T(8,128)(2,1)}, bf16[256,256]{1,0:T(8,128)(2,1)S(1)}, u32[]{:S(2)}, u32[]{:S(2)}) collective-permute-start(bf16[256,256]{1,0:T(8,128)(2,1)} %get-tuple-element.64), channel_id=1, source_target_pairs={{0,32},{32,64},{64,96},{96,0},{1,33},{33,65},{65,97},{97,1},{2,34}... | collective-permute-start | bytes 393224 | tf_op jit(solution)/shard_map/ppermute | solution.py:350
  101.9 16.3 %all-to-all-start.3 = ((bf16[16,96,256]{2,1,0:T(8,128)(2,1)}), bf16[16,96,256]{2,1,0:T(8,128)(2,1)S(1)}, u32[]{:S(2)}, u32[]{:S(2)}) async-start(bf16[16,96,256]{2,1,0:T(8,128)(2,1)} %get-tuple-element.67), calls=%async_computation.3 | async-start | bytes 1572864 | tf_op jit(solution)/shard_map/all_to_all | solution.py:358
  134.1 20.5 %all-to-all-start.4 = ((bf16[16,96,256]{2,1,0:T(8,128)(2,1)}), bf16[16,96,256]{2,1,0:T(8,128)(2,1)S(1)}, u32[]{:S(2)}, u32[]{:S(2)}) async-start(bf16[16,96,256]{2,1,0:T(8,128)(2,1)} %bitcast.38), calls=%async_computation.4 | async-start | bytes 1572864 | tf_op jit(solution)/shard_map/all_to_all | solution.py:358
  137.7 7.3 %collective-permute-start.22 = (bf16[544,256]{1,0:T(8,128)(2,1)}, bf16[544,256]{1,0:T(8,128)(2,1)S(1)}, u32[]{:S(2)}, u32[]{:S(2)}) collective-permute-start(bf16[544,256]{1,0:T(8,128)(2,1)} %get-tuple-element.77), channel_id=1, source_target_pairs={{0,64},{32,96},{64,0},{96,32},{1,65},{33,97},{65,1},{97,33},{2,66}... | collective-permute-start | bytes 835592 | tf_op jit(solution)/shard_map/ppermute | solution.py:350
  139.7 12.7 %collective-permute-start.23 = (bf16[544,256]{1,0:T(8,128)(2,1)}, bf16[544,256]{1,0:T(8,128)(2,1)S(1)}, u32[]{:S(2)}, u32[]{:S(2)}) collective-permute-start(bf16[544,256]{1,0:T(8,128)(2,1)} %get-tuple-element.78), channel_id=1, source_target_pairs={{0,96},{32,0},{64,32},{96,64},{1,97},{33,1},{65,33},{97,65},{2,98}... | collective-permute-start | bytes 835592 | tf_op jit(solution)/shard_map/ppermute | solution.py:350
  140.2 14.3 %collective-permute-start.24 = (bf16[544,256]{1,0:T(8,128)(2,1)}, bf16[544,256]{1,0:T(8,128)(2,1)S(1)}, u32[]{:S(2)}, u32[]{:S(2)}) collective-permute-start(bf16[544,256]{1,0:T(8,128)(2,1)} %get-tuple-element.79), channel_id=1, source_target_pairs={{0,32},{32,64},{64,96},{96,0},{1,33},{33,65},{65,97},{97,1},{2,34}... | collective-permute-start | bytes 835592 | tf_op jit(solution)/shard_map/ppermute | solution.py:350
  141.2 14.0 %collective-permute-start.25 = (bf16[544,256]{1,0:T(8,128)(2,1)}, bf16[544,256]{1,0:T(8,128)(2,1)S(1)}, u32[]{:S(2)}, u32[]{:S(2)}) collective-permute-start(bf16[544,256]{1,0:T(8,128)(2,1)} %get-tuple-element.76.refs_0_), channel_id=1, source_target_pairs={{0,1},{1,0},{2,3},{3,2},{4,5},{5,4},{6,7},{7,6},{8,9},{9,8},{10,11... | collective-permute-start | bytes 835592 | tf_op jit(solution)/shard_map/ppermute | solution.py:354
  145.0 10.2 %collective-permute-start.26 = (bf16[544,256]{1,0:T(8,128)(2,1)S(1)}, bf16[544,256]{1,0:T(8,128)(2,1)S(1)}, u32[]{:S(2)}, u32[]{:S(2)}) collective-permute-start(bf16[544,256]{1,0:T(8,128)(2,1)S(1)} %collective-permute-done.22.refs_1_), channel_id=1, source_target_pairs={{0,1},{1,0},{2,3},{3,2},{4,5},{5,4},{6,7},{7,6},{8,9},{9,8},{10,11... | collective-permute-start | bytes 835592 | tf_op jit(solution)/shard_map/ppermute | solution.py:354
  154.7 4.0 %collective-permute-start.21 = (f32[3,16,256]{2,1,0:T(8,128)S(1)}, f32[3,16,256]{2,1,0:T(8,128)S(1)}, u32[]{:S(2)}, u32[]{:S(2)}) collective-permute-start(f32[3,16,256]{2,1,0:T(8,128)S(1)} %dynamic-slice_bitcast_fusion), channel_id=1, source_target_pairs={{0,1},{1,0},{2,3},{3,2},{4,5},{5,4},{6,7},{7,6},{8,9},{9,8},{10,11... | collective-permute-start | bytes 147464 | tf_op jit(solution)/shard_map/ppermute | solution.py:460
  (35 other events, 190.2 us)

commit v2 on v1

--- a/solution.py
+++ b/solution.py
@@ -139,7 +139,7 @@
 
 
 def give(refs, value, start, rows):
-    rounded = value.T.astype(BF16)
+    rounded = value.astype(BF16).T
     for slot, ref in enumerate(refs):
         ref[start : start + rows] = rounded[slot * rows : (slot + 1) * rows]
 
@@ -180,7 +180,10 @@
 
 
 def inner_kernel(rows, *refs):
-    sources, (wh_ref, wl_ref, out_ref, acc_ref, p_ref, x_ref) = refs[:-6], refs[-6:]
+    sources, rest = refs[:-7], refs[-7:]
+    w_ref, out_ref, acc_ref, p_ref, x_ref, wh_ref, wl_ref = rest
+    for index in range(3):
+        wh_ref[index], wl_ref[index] = halves(w_ref[index])
     messages = pieces(sources[: len(sources) // 2], sources[len(sources) // 2 :])
     for step, group in groups_of(messages):
         put = functools.partial(add_to, acc_ref, out_ref, step)
@@ -391,10 +394,10 @@
         part_shape,
         flops=12 * product,
         vmem=60,
-        in_specs=[memory] * (heads + 2),
+        in_specs=[memory] * (heads + 1),
         out_specs=memory,
-        scratch_shapes=scratch + [products, half_terms],
-    )(*kv, w_high, w_low)
+        scratch_shapes=scratch + [products, half_terms] + [pltpu.VMEM((3, hid, width), BF16)] * 2,
+    )(*kv, weights)
     own_shape = shape((3 * share, width), F32)
     spread_shape = shape((owners, 3 * share, width), BF16)
     summed, qg[1] = lax.optimization_barrier((scatter(grad_part), qg[1]))
@@ -447,12 +450,6 @@
         ],
     )(*kv, w_high, w_low, cotangent)
     d_kv = along(d_kv, -1)
-    key_grad, value_grad, step_grad = call(
-        unpack_kv_kernel,
-        (shape(wide, BF16), shape(wide, BF16), shape((heads, rows), BF16)),
-        in_specs=taken,
-    )(places, *d_kv, *across(d_kv))
-    step_grad = step_grad.T
     summed = call(last_kernel, own_shape)(scatter(second_part), direct)
     summed = summed.reshape(3, 2, share // 2, width)
     kept = lax.dynamic_index_in_dim(summed, core, 1, keepdims=False)
@@ -460,6 +457,13 @@
     got = lax.ppermute(sent, "c", [(0, 1), (1, 0)])
     first = core == 0
     meta_grad = jnp.stack([jnp.where(first, kept, got), jnp.where(first, got, kept)])
+    got, meta_grad = lax.optimization_barrier((across(d_kv), meta_grad))
+    key_grad, value_grad, step_grad = call(
+        unpack_kv_kernel,
+        (shape(wide, BF16), shape(wide, BF16), shape((heads, rows), BF16)),
+        in_specs=taken,
+    )(places, *d_kv, *got)
+    step_grad = step_grad.T
     return meta_grad, query_grad, key_grad, value_grad, step_grad
 
 

time: 160 us -> 159 us (level)
  starting transfers between devices: 67.5 us -> 59.4 us
  waiting for transfers between devices: 42.9 us -> 49.6 us
    ppermute x16, starting transfers between devices: 24.4 us -> 13.1 us  [across(): lax.ppermute(message, 'c', [(0, 1), (1, 0)])]
    all_to_all x5, waiting for transfers between devices: 16.5 us -> 25 us  [scatter(): return lax.all_to_all(message, 'p', 0, 0, tiled=True)]
    ppermute x1, starting transfers between devices: 0.55 us -> 3.66 us  [body(): got = lax.ppermute(sent, 'c', [(0, 1), (1, 0)])]
    convert_element_type x1 -> x2, other arithmetic: 2.81 us -> 4.08 us  [body(): w_high, w_low = (rounded.astype(BF16), (weights - rounded).astype(BF16))]
    unnamed x50 -> x64, local copies, waits for them, and re-layouts: 6.48 us -> 5.55 us
  transfers between devices with their start and end apart: 34 -> 34, of which waited for: 22 -> 19; matrix products, arithmetic and copies ran while one was open for 2% -> 4% of each run, Pallas kernels for 2% -> 1%
where the time goes in v2:
time: 159 us; the launch traced here: 158 us
  starting transfers between devices  59.4 us (37%)
  waiting for transfers between devices  49.6 us (31%)
  Pallas kernels  37 us (23%)
  local copies, waits for them, and re-layouts  6.56 us (4%)
  other arithmetic  4.74 us (3%)
    all_to_all x5, waiting for transfers between devices, scatter(): return lax.all_to_all(message, 'p', 0, 0, tiled=True)  25 us
    all_to_all x5, starting transfers between devices, scatter(): return lax.all_to_all(message, 'p', 0, 0, tiled=True)  24 us
    ppermute x12, waiting for transfers between devices, along(): lax.ppermute(m, 'z', pair)  21.9 us
    ppermute x12, starting transfers between devices, along(): lax.ppermute(m, 'z', pair)  18.7 us
    pallas_call x1, Pallas kernels, body(): call(functools.partial(second_kernel, rows), messages_of(2 * rows + PAD)...  15 us
    ppermute x16, starting transfers between devices, across(): lax.ppermute(message, 'c', [(0, 1), (1, 0)])  13.1 us
    pallas_call x1, Pallas kernels, body(): call(functools.partial(outer_kernel, rows), messages_of(rows) + (part_sha...  7.98 us
    pallas_call x1, Pallas kernels, body(): call(functools.partial(inner_kernel, rows), part_shape, flops=12 * produc...  7.27 us
  transfers between devices with their start and end apart: 34, of which 19 were waited for; matrix products, arithmetic and copies ran while one was open for 4% of the time, Pallas kernels for 1%

profile of v2, /device:TPU:1, one launch (start us, length us, event | category | flops | bytes accessed | tf_op | source)
XLA Modules:
  0.0 158.4 jit_solution(9561237672061891485)
XLA Ops:
  4.2 4.5 %collective-permute-start = (bf16[544,256]{1,0:T(8,128)(2,1)S(1)}, bf16[544,256]{1,0:T(8,128)(2,1)S(1)}, u32[]{:S(2)}, u32[]{:S(2)}) collective-permute-start(bf16[544,256]{1,0:T(8,128)(2,1)S(1)} %get-tuple-element.50), channel_id=1, source_target_pairs={{0,64},{32,96},{64,0},{96,32},{1,65},{33,97},{65,1},{97,33},{2,66}... | collective-permute-start | bytes 835592 | tf_op jit(solution)/shard_map/ppermute | solution.py:353
  12.9 2.2 %collective-permute-done.refs_1_ = bf16[544,256]{1,0:T(8,128)(2,1)S(1)} collective-permute-done((bf16[544,256]{1,0:T(8,128)(2,1)S(1)}, bf16[544,256]{1,0:T(8,128)(2,1)S(1)}, u32[]{:S(2)}, u32[]{:S(2)}) %collective-permute-start) | collective-permute-done | bytes 278560 | tf_op jit(solution)/shard_map/ppermute | solution.py:353
  15.2 2.1 %collective-permute-start.4 = (bf16[544,256]{1,0:T(8,128)(2,1)S(1)}, bf16[544,256]{1,0:T(8,128)(2,1)S(1)}, u32[]{:S(2)}, u32[]{:S(2)}) collective-permute-start(bf16[544,256]{1,0:T(8,128)(2,1)S(1)} %collective-permute-done.refs_1_), channel_id=1, source_target_pairs={{0,1},{1,0},{2,3},{3,2},{4,5},{5,4},{6,7},{7,6},{8,9},{9,8},{10,11... | collective-permute-start | bytes 835592 | tf_op jit(solution)/shard_map/ppermute | solution.py:357
  17.2 4.6 %collective-permute-done.1.refs_2_ = bf16[544,256]{1,0:T(8,128)(2,1)S(1)} collective-permute-done((bf16[544,256]{1,0:T(8,128)(2,1)S(1)}, bf16[544,256]{1,0:T(8,128)(2,1)S(1)}, u32[]{:S(2)}, u32[]{:S(2)}) %collective-permute-start.1) | collective-permute-done | bytes 278560 | tf_op jit(solution)/shard_map/ppermute | solution.py:353
  23.1 3.1 %fusion = (bf16[3,512,256]{2,1,0:T(8,128)(2,1)}, f32[3,512,256]{2,1,0:T(8,128)}) fusion(f32[2,3,512,256]{3,2,1,0:T(8,128)} %param.10, s32[]{:T(128)S(6)} %select_n.81), kind=kLoop, calls=%fused_computation.2 | loop fusion | flops 1179648 | bytes 3932164 | tf_op jit(solution)/shard_map/convert_element_type | solution.py:366
  27.2 7.3 %shard_map.103 = bf16[16,3,32,256]{3,2,1,0:T(8,128)(2,1)} custom-call(bf16[544,256]{1,0:T(8,128)(2,1)} %copy-done.7, bf16[544,256]{1,0:T(8,128)(2,1)} %copy-done.12, bf16[544,256]{1,0:T(8,128)(2,1)} %copy-done.13, bf16[544,256]{1,0:T(8,128)(2,1)} %copy-done.14, bf16[544,256]{1,0:T(8,128)(2,1)} %copy-done.15, bf16[544,256]{1,0:T(8,128)(2,1)} %copy-done.16, ...), custom_call_target="tpu_custom_call" | custom-call | flops 3221225472 | bytes 4194304 | tf_op jit(solution)/shard_map/pallas_call | solution.py:392
  34.5 6.9 %all-to-all-start = ((bf16[16,96,256]{2,1,0:T(8,128)(2,1)}), bf16[16,96,256]{2,1,0:T(8,128)(2,1)S(1)}, u32[]{:S(2)}, u32[]{:S(2)}) async-start(bf16[16,96,256]{2,1,0:T(8,128)(2,1)} %bitcast.40), calls=%async_computation | async-start | bytes 1572864 | tf_op jit(solution)/shard_map/all_to_all | solution.py:361
  45.0 6.3 %collective-permute-done.7.refs_1_ = bf16[512,256]{1,0:T(8,128)(2,1)S(1)} collective-permute-done((bf16[512,256]{1,0:T(8,128)(2,1)S(1)}, bf16[512,256]{1,0:T(8,128)(2,1)S(1)}, u32[]{:S(2)}, u32[]{:S(2)}) %collective-permute-start.7) | collective-permute-done | bytes 262176 | tf_op jit(solution)/shard_map/ppermute | solution.py:353
  51.3 4.0 %all-to-all-done.in_ref = bf16[16,96,256]{2,1,0:T(8,128)(2,1)S(1)} async-done(((bf16[16,96,256]{2,1,0:T(8,128)(2,1)}), bf16[16,96,256]{2,1,0:T(8,128)(2,1)S(1)}, u32[]{:S(2)}, u32[]{:S(2)}) %all-to-all-start) | async-done | bytes 786464 | tf_op jit(solution)/shard_map/all_to_all | solution.py:361
  56.4 3.7 %all-to-all-start.1 = ((bf16[16,96,256]{2,1,0:T(8,128)(2,1)}), bf16[16,96,256]{2,1,0:T(8,128)(2,1)S(1)}, u32[]{:S(2)}, u32[]{:S(2)}) async-start(bf16[16,96,256]{2,1,0:T(8,128)(2,1)} %get-tuple-element.59), calls=%async_computation.1 | async-start | bytes 1572864 | tf_op jit(solution)/shard_map/all_to_all | solution.py:361
  60.6 2.2 %collective-permute-start.9 = (bf16[512,256]{1,0:T(8,128)(2,1)S(1)}, bf16[512,256]{1,0:T(8,128)(2,1)S(1)}, u32[]{:S(2)}, u32[]{:S(2)}) collective-permute-start(bf16[512,256]{1,0:T(8,128)(2,1)S(1)} %get-tuple-element.57), channel_id=1, source_target_pairs={{0,96},{32,0},{64,32},{96,64},{1,97},{33,1},{65,33},{97,65},{2,98}... | collective-permute-start | bytes 786440 | tf_op jit(solution)/shard_map/ppermute | solution.py:353
  64.8 3.0 %collective-permute-done.8.refs_2_ = bf16[512,256]{1,0:T(8,128)(2,1)S(1)} collective-permute-done((bf16[512,256]{1,0:T(8,128)(2,1)S(1)}, bf16[512,256]{1,0:T(8,128)(2,1)S(1)}, u32[]{:S(2)}, u32[]{:S(2)}) %collective-permute-start.8) | collective-permute-done | bytes 262176 | tf_op jit(solution)/shard_map/ppermute | solution.py:353
  67.7 2.3 %collective-permute-start.12 = (bf16[512,256]{1,0:T(8,128)(2,1)S(1)}, bf16[512,256]{1,0:T(8,128)(2,1)S(1)}, u32[]{:S(2)}, u32[]{:S(2)}) collective-permute-start(bf16[512,256]{1,0:T(8,128)(2,1)S(1)} %collective-permute-done.8.refs_2_), channel_id=1, source_target_pairs={{0,1},{1,0},{2,3},{3,2},{4,5},{5,4},{6,7},{7,6},{8,9},{9,8},{10,11... | collective-permute-start | bytes 786440 | tf_op jit(solution)/shard_map/ppermute | solution.py:357
  73.7 8.0 %shard_map.105 = (bf16[256,256]{1,0:T(8,128)(2,1)}, bf16[256,256]{1,0:T(8,128)(2,1)}, bf16[256,256]{1,0:T(8,128)(2,1)}, bf16[256,256]{1,0:T(8,128)(2,1)}, bf16[16,3,32,256]{3,2,1,0:T(8,128)(2,1)}) custom-call(bf16[512,256]{1,0:T(8,128)(2,1)} %copy-done.8, bf16[512,256]{1,0:T(8,128)(2,1)} %copy-done.22, bf16[512,256]{1,0:T(8,128)(2,1)} %copy-done.23, ...), custom_call_target="tpu_custom_call" | custom-call | flops 3489660928 | bytes 4194304 | tf_op jit(solution)/shard_map/pallas_call | solution.py:407
  81.7 6.0 %all-to-all-start.2 = ((bf16[16,96,256]{2,1,0:T(8,128)(2,1)}), bf16[16,96,256]{2,1,0:T(8,128)(2,1)S(1)}, u32[]{:S(2)}, u32[]{:S(2)}) async-start(bf16[16,96,256]{2,1,0:T(8,128)(2,1)} %bitcast.42), calls=%async_computation.2 | async-start | bytes 1572864 | tf_op jit(solution)/shard_map/all_to_all | solution.py:361
  91.2 2.6 %collective-permute-done.14.refs_1_ = bf16[256,256]{1,0:T(8,128)(2,1)S(1)} collective-permute-done((bf16[256,256]{1,0:T(8,128)(2,1)S(1)}, bf16[256,256]{1,0:T(8,128)(2,1)S(1)}, u32[]{:S(2)}, u32[]{:S(2)}) %collective-permute-start.14) | collective-permute-done | bytes 131104 | tf_op jit(solution)/shard_map/ppermute | solution.py:353
  93.8 2.8 %collective-permute-done.15.refs_2_ = bf16[256,256]{1,0:T(8,128)(2,1)S(1)} collective-permute-done((bf16[256,256]{1,0:T(8,128)(2,1)S(1)}, bf16[256,256]{1,0:T(8,128)(2,1)S(1)}, u32[]{:S(2)}, u32[]{:S(2)}) %collective-permute-start.15) | collective-permute-done | bytes 131104 | tf_op jit(solution)/shard_map/ppermute | solution.py:353
  97.0 4.3 %all-to-all-done.2.in_ref = bf16[16,96,256]{2,1,0:T(8,128)(2,1)S(1)} async-done(((bf16[16,96,256]{2,1,0:T(8,128)(2,1)}), bf16[16,96,256]{2,1,0:T(8,128)(2,1)S(1)}, u32[]{:S(2)}, u32[]{:S(2)}) %all-to-all-start.2) | async-done | bytes 786464 | tf_op jit(solution)/shard_map/all_to_all | solution.py:361
  102.4 3.6 %all-to-all-start.3 = ((bf16[16,96,256]{2,1,0:T(8,128)(2,1)}), bf16[16,96,256]{2,1,0:T(8,128)(2,1)S(1)}, u32[]{:S(2)}, u32[]{:S(2)}) async-start(bf16[16,96,256]{2,1,0:T(8,128)(2,1)} %get-tuple-element.72), calls=%async_computation.3 | async-start | bytes 1572864 | tf_op jit(solution)/shard_map/all_to_all | solution.py:361
  111.1 7.6 %all-to-all-done.3 = bf16[16,96,256]{2,1,0:T(8,128)(2,1)S(1)} async-done(((bf16[16,96,256]{2,1,0:T(8,128)(2,1)}), bf16[16,96,256]{2,1,0:T(8,128)(2,1)S(1)}, u32[]{:S(2)}, u32[]{:S(2)}) %all-to-all-start.3) | async-done | bytes 786464 | tf_op jit(solution)/shard_map/all_to_all | solution.py:361
  119.6 15.0 %shard_map.108 = (bf16[544,256]{1,0:T(8,128)(2,1)}, bf16[544,256]{1,0:T(8,128)(2,1)}, bf16[544,256]{1,0:T(8,128)(2,1)}, bf16[544,256]{1,0:T(8,128)(2,1)}, bf16[16,3,32,256]{3,2,1,0:T(8,128)(2,1)}) custom-call(bf16[544,256]{1,0:T(8,128)(2,1)} %copy-done.7, bf16[544,256]{1,0:T(8,128)(2,1)} %copy-done.12, bf16[544,256]{1,0:T(8,128)(2,1)} %copy-done.13, ...), custom_call_target="tpu_custom_call" | custom-call | flops 6442450944 | bytes 4194304 | tf_op jit(solution)/shard_map/pallas_call | solution.py:432
  134.7 3.8 %all-to-all-start.4 = ((bf16[16,96,256]{2,1,0:T(8,128)(2,1)}), bf16[16,96,256]{2,1,0:T(8,128)(2,1)S(1)}, u32[]{:S(2)}, u32[]{:S(2)}) async-start(bf16[16,96,256]{2,1,0:T(8,128)(2,1)} %bitcast.41), calls=%async_computation.4 | async-start | bytes 1572864 | tf_op jit(solution)/shard_map/all_to_all | solution.py:361
  141.8 8.4 %all-to-all-done.4.in_ref = bf16[16,96,256]{2,1,0:T(8,128)(2,1)S(1)} async-done(((bf16[16,96,256]{2,1,0:T(8,128)(2,1)}), bf16[16,96,256]{2,1,0:T(8,128)(2,1)S(1)}, u32[]{:S(2)}, u32[]{:S(2)}) %all-to-all-start.4) | async-done | bytes 786464 | tf_op jit(solution)/shard_map/all_to_all | solution.py:361
  150.3 3.7 %collective-permute-start.28 = (f32[3,16,256]{2,1,0:T(8,128)S(1)}, f32[3,16,256]{2,1,0:T(8,128)S(1)}, u32[]{:S(2)}, u32[]{:S(2)}) collective-permute-start(f32[3,16,256]{2,1,0:T(8,128)S(1)} %dynamic-slice_bitcast_fusion.1), channel_id=1, source_target_pairs={{0,1},{1,0},{2,3},{3,2},{4,5},{5,4},{6,7},{7,6},{8,9},{9,8},{10,11... | collective-permute-start | bytes 147464 | tf_op jit(solution)/shard_map/ppermute | solution.py:457
  (125 shorter events, 39.6 us)
Async XLA Ops:
  4.2 10.9 %collective-permute-start = (bf16[544,256]{1,0:T(8,128)(2,1)S(1)}, bf16[544,256]{1,0:T(8,128)(2,1)S(1)}, u32[]{:S(2)}, u32[]{:S(2)}) collective-permute-start(bf16[544,256]{1,0:T(8,128)(2,1)S(1)} %get-tuple-element.50), channel_id=1, source_target_pairs={{0,64},{32,96},{64,0},{96,32},{1,65},{33,97},{65,1},{97,33},{2,66}... | collective-permute-start | bytes 835592 | tf_op jit(solution)/shard_map/ppermute | solution.py:353
  8.8 13.1 %collective-permute-start.1 = (bf16[544,256]{1,0:T(8,128)(2,1)S(1)}, bf16[544,256]{1,0:T(8,128)(2,1)S(1)}, u32[]{:S(2)}, u32[]{:S(2)}) collective-permute-start(bf16[544,256]{1,0:T(8,128)(2,1)S(1)} %get-tuple-element.51), channel_id=1, source_target_pairs={{0,32},{32,64},{64,96},{96,0},{1,33},{33,65},{65,97},{97,1},{2,34}... | collective-permute-start | bytes 835592 | tf_op jit(solution)/shard_map/ppermute | solution.py:353
  9.5 12.8 %collective-permute-start.2 = (bf16[544,256]{1,0:T(8,128)(2,1)S(1)}, bf16[544,256]{1,0:T(8,128)(2,1)S(1)}, u32[]{:S(2)}, u32[]{:S(2)}) collective-permute-start(bf16[544,256]{1,0:T(8,128)(2,1)S(1)} %get-tuple-element.52), channel_id=1, source_target_pairs={{0,96},{32,0},{64,32},{96,64},{1,97},{33,1},{65,33},{97,65},{2,98}... | collective-permute-start | bytes 835592 | tf_op jit(solution)/shard_map/ppermute | solution.py:353
  11.4 14.8 %collective-permute-start.3 = (bf16[544,256]{1,0:T(8,128)(2,1)S(1)}, bf16[544,256]{1,0:T(8,128)(2,1)S(1)}, u32[]{:S(2)}, u32[]{:S(2)}) collective-permute-start(bf16[544,256]{1,0:T(8,128)(2,1)S(1)} %get-tuple-element.49.refs_0_), channel_id=1, source_target_pairs={{0,1},{1,0},{2,3},{3,2},{4,5},{5,4},{6,7},{7,6},{8,9},{9,8},{10,11... | collective-permute-start | bytes 835592 | tf_op jit(solution)/shard_map/ppermute | solution.py:357
  15.2 11.0 %collective-permute-start.4 = (bf16[544,256]{1,0:T(8,128)(2,1)S(1)}, bf16[544,256]{1,0:T(8,128)(2,1)S(1)}, u32[]{:S(2)}, u32[]{:S(2)}) collective-permute-start(bf16[544,256]{1,0:T(8,128)(2,1)S(1)} %collective-permute-done.refs_1_), channel_id=1, source_target_pairs={{0,1},{1,0},{2,3},{3,2},{4,5},{5,4},{6,7},{7,6},{8,9},{9,8},{10,11... | collective-permute-start | bytes 835592 | tf_op jit(solution)/shard_map/ppermute | solution.py:357
  21.8 4.4 %collective-permute-start.5 = (bf16[544,256]{1,0:T(8,128)(2,1)S(1)}, bf16[544,256]{1,0:T(8,128)(2,1)S(1)}, u32[]{:S(2)}, u32[]{:S(2)}) collective-permute-start(bf16[544,256]{1,0:T(8,128)(2,1)S(1)} %collective-permute-done.1.refs_2_), channel_id=1, source_target_pairs={{0,1},{1,0},{2,3},{3,2},{4,5},{5,4},{6,7},{7,6},{8,9},{9,8},{10,11... | collective-permute-start | bytes 835592 | tf_op jit(solution)/shard_map/ppermute | solution.py:357
  22.3 3.9 %collective-permute-start.6 = (bf16[544,256]{1,0:T(8,128)(2,1)S(1)}, bf16[544,256]{1,0:T(8,128)(2,1)S(1)}, u32[]{:S(2)}, u32[]{:S(2)}) collective-permute-start(bf16[544,256]{1,0:T(8,128)(2,1)S(1)} %collective-permute-done.2.refs_3_), channel_id=1, source_target_pairs={{0,1},{1,0},{2,3},{3,2},{4,5},{5,4},{6,7},{7,6},{8,9},{9,8},{10,11... | collective-permute-start | bytes 835592 | tf_op jit(solution)/shard_map/ppermute | solution.py:357
  34.5 20.7 %all-to-all-start = ((bf16[16,96,256]{2,1,0:T(8,128)(2,1)}), bf16[16,96,256]{2,1,0:T(8,128)(2,1)S(1)}, u32[]{:S(2)}, u32[]{:S(2)}) async-start(bf16[16,96,256]{2,1,0:T(8,128)(2,1)} %bitcast.40), calls=%async_computation | async-start | bytes 1572864 | tf_op jit(solution)/shard_map/all_to_all | solution.py:361
  42.2 9.1 %collective-permute-start.7 = (bf16[512,256]{1,0:T(8,128)(2,1)S(1)}, bf16[512,256]{1,0:T(8,128)(2,1)S(1)}, u32[]{:S(2)}, u32[]{:S(2)}) collective-permute-start(bf16[512,256]{1,0:T(8,128)(2,1)S(1)} %get-tuple-element.54), channel_id=1, source_target_pairs={{0,64},{32,96},{64,0},{96,32},{1,65},{33,97},{65,1},{97,33},{2,66}... | collective-permute-start | bytes 786440 | tf_op jit(solution)/shard_map/ppermute | solution.py:353
  56.4 16.5 %all-to-all-start.1 = ((bf16[16,96,256]{2,1,0:T(8,128)(2,1)}), bf16[16,96,256]{2,1,0:T(8,128)(2,1)S(1)}, u32[]{:S(2)}, u32[]{:S(2)}) async-start(bf16[16,96,256]{2,1,0:T(8,128)(2,1)} %get-tuple-element.59), calls=%async_computation.1 | async-start | bytes 1572864 | tf_op jit(solution)/shard_map/all_to_all | solution.py:361
  60.1 7.7 %collective-permute-start.8 = (bf16[512,256]{1,0:T(8,128)(2,1)S(1)}, bf16[512,256]{1,0:T(8,128)(2,1)S(1)}, u32[]{:S(2)}, u32[]{:S(2)}) collective-permute-start(bf16[512,256]{1,0:T(8,128)(2,1)S(1)} %get-tuple-element.56), channel_id=1, source_target_pairs={{0,32},{32,64},{64,96},{96,0},{1,33},{33,65},{65,97},{97,1},{2,34}... | collective-permute-start | bytes 786440 | tf_op jit(solution)/shard_map/ppermute | solution.py:353
  60.6 9.5 %collective-permute-start.9 = (bf16[512,256]{1,0:T(8,128)(2,1)S(1)}, bf16[512,256]{1,0:T(8,128)(2,1)S(1)}, u32[]{:S(2)}, u32[]{:S(2)}) collective-permute-start(bf16[512,256]{1,0:T(8,128)(2,1)S(1)} %get-tuple-element.57), channel_id=1, source_target_pairs={{0,96},{32,0},{64,32},{96,64},{1,97},{33,1},{65,33},{97,65},{2,98}... | collective-permute-start | bytes 786440 | tf_op jit(solution)/shard_map/ppermute | solution.py:353
  62.8 7.8 %collective-permute-start.10 = (bf16[512,256]{1,0:T(8,128)(2,1)S(1)}, bf16[512,256]{1,0:T(8,128)(2,1)S(1)}, u32[]{:S(2)}, u32[]{:S(2)}) collective-permute-start(bf16[512,256]{1,0:T(8,128)(2,1)S(1)} %get-tuple-element.53.refs_0_), channel_id=1, source_target_pairs={{0,1},{1,0},{2,3},{3,2},{4,5},{5,4},{6,7},{7,6},{8,9},{9,8},{10,11... | collective-permute-start | bytes 786440 | tf_op jit(solution)/shard_map/ppermute | solution.py:357
  67.7 3.5 %collective-permute-start.12 = (bf16[512,256]{1,0:T(8,128)(2,1)S(1)}, bf16[512,256]{1,0:T(8,128)(2,1)S(1)}, u32[]{:S(2)}, u32[]{:S(2)}) collective-permute-start(bf16[512,256]{1,0:T(8,128)(2,1)S(1)} %collective-permute-done.8.refs_2_), channel_id=1, source_target_pairs={{0,1},{1,0},{2,3},{3,2},{4,5},{5,4},{6,7},{7,6},{8,9},{9,8},{10,11... | collective-permute-start | bytes 786440 | tf_op jit(solution)/shard_map/ppermute | solution.py:357
  81.7 19.5 %all-to-all-start.2 = ((bf16[16,96,256]{2,1,0:T(8,128)(2,1)}), bf16[16,96,256]{2,1,0:T(8,128)(2,1)S(1)}, u32[]{:S(2)}, u32[]{:S(2)}) async-start(bf16[16,96,256]{2,1,0:T(8,128)(2,1)} %bitcast.42), calls=%async_computation.2 | async-start | bytes 1572864 | tf_op jit(solution)/shard_map/all_to_all | solution.py:361
  87.8 6.0 %collective-permute-start.14 = (bf16[256,256]{1,0:T(8,128)(2,1)S(1)}, bf16[256,256]{1,0:T(8,128)(2,1)S(1)}, u32[]{:S(2)}, u32[]{:S(2)}) collective-permute-start(bf16[256,256]{1,0:T(8,128)(2,1)S(1)} %copy-done.31), channel_id=1, source_target_pairs={{0,64},{32,96},{64,0},{96,32},{1,65},{33,97},{65,1},{97,33},{2,66}... | collective-permute-start | bytes 393224 | tf_op jit(solution)/shard_map/ppermute | solution.py:353
  89.7 6.8 %collective-permute-start.15 = (bf16[256,256]{1,0:T(8,128)(2,1)S(1)}, bf16[256,256]{1,0:T(8,128)(2,1)S(1)}, u32[]{:S(2)}, u32[]{:S(2)}) collective-permute-start(bf16[256,256]{1,0:T(8,128)(2,1)S(1)} %copy-done.30), channel_id=1, source_target_pairs={{0,96},{32,0},{64,32},{96,64},{1,97},{33,1},{65,33},{97,65},{2,98}... | collective-permute-start | bytes 393224 | tf_op jit(solution)/shard_map/ppermute | solution.py:353
  90.3 6.7 %collective-permute-start.16 = (bf16[256,256]{1,0:T(8,128)(2,1)S(1)}, bf16[256,256]{1,0:T(8,128)(2,1)S(1)}, u32[]{:S(2)}, u32[]{:S(2)}) collective-permute-start(bf16[256,256]{1,0:T(8,128)(2,1)S(1)} %copy-done.29), channel_id=1, source_target_pairs={{0,32},{32,64},{64,96},{96,0},{1,33},{33,65},{65,97},{97,1},{2,34}... | collective-permute-start | bytes 393224 | tf_op jit(solution)/shard_map/ppermute | solution.py:353
  102.4 16.3 %all-to-all-start.3 = ((bf16[16,96,256]{2,1,0:T(8,128)(2,1)}), bf16[16,96,256]{2,1,0:T(8,128)(2,1)S(1)}, u32[]{:S(2)}, u32[]{:S(2)}) async-start(bf16[16,96,256]{2,1,0:T(8,128)(2,1)} %get-tuple-element.72), calls=%async_computation.3 | async-start | bytes 1572864 | tf_op jit(solution)/shard_map/all_to_all | solution.py:361
  134.7 15.5 %all-to-all-start.4 = ((bf16[16,96,256]{2,1,0:T(8,128)(2,1)}), bf16[16,96,256]{2,1,0:T(8,128)(2,1)S(1)}, u32[]{:S(2)}, u32[]{:S(2)}) async-start(bf16[16,96,256]{2,1,0:T(8,128)(2,1)} %bitcast.41), calls=%async_computation.4 | async-start | bytes 1572864 | tf_op jit(solution)/shard_map/all_to_all | solution.py:361
  138.4 15.7 %collective-permute-start.22 = (bf16[544,256]{1,0:T(8,128)(2,1)S(1)}, bf16[544,256]{1,0:T(8,128)(2,1)S(1)}, u32[]{:S(2)}, u32[]{:S(2)}) collective-permute-start(bf16[544,256]{1,0:T(8,128)(2,1)S(1)} %copy-done.21), channel_id=1, source_target_pairs={{0,64},{32,96},{64,0},{96,32},{1,65},{33,97},{65,1},{97,33},{2,66}... | collective-permute-start | bytes 835592 | tf_op jit(solution)/shard_map/ppermute | solution.py:353
  140.4 14.1 %collective-permute-start.24 = (bf16[544,256]{1,0:T(8,128)(2,1)S(1)}, bf16[544,256]{1,0:T(8,128)(2,1)S(1)}, u32[]{:S(2)}, u32[]{:S(2)}) collective-permute-start(bf16[544,256]{1,0:T(8,128)(2,1)S(1)} %copy-done.20), channel_id=1, source_target_pairs={{0,96},{32,0},{64,32},{96,64},{1,97},{33,1},{65,33},{97,65},{2,98}... | collective-permute-start | bytes 835592 | tf_op jit(solution)/shard_map/ppermute | solution.py:353
  140.9 14.1 %collective-permute-start.26 = (bf16[544,256]{1,0:T(8,128)(2,1)S(1)}, bf16[544,256]{1,0:T(8,128)(2,1)S(1)}, u32[]{:S(2)}, u32[]{:S(2)}) collective-permute-start(bf16[544,256]{1,0:T(8,128)(2,1)S(1)} %copy-done.19), channel_id=1, source_target_pairs={{0,32},{32,64},{64,96},{96,0},{1,33},{33,65},{65,97},{97,1},{2,34}... | collective-permute-start | bytes 835592 | tf_op jit(solution)/shard_map/ppermute | solution.py:353
  150.3 4.7 %collective-permute-start.28 = (f32[3,16,256]{2,1,0:T(8,128)S(1)}, f32[3,16,256]{2,1,0:T(8,128)S(1)}, u32[]{:S(2)}, u32[]{:S(2)}) collective-permute-start(f32[3,16,256]{2,1,0:T(8,128)S(1)} %dynamic-slice_bitcast_fusion.1), channel_id=1, source_target_pairs={{0,1},{1,0},{2,3},{3,2},{4,5},{5,4},{6,7},{7,6},{8,9},{9,8},{10,11... | collective-permute-start | bytes 147464 | tf_op jit(solution)/shard_map/ppermute | solution.py:457
  (42 other events, 244.4 us)

commit v3 on v2

--- a/solution.py
+++ b/solution.py
@@ -111,16 +111,6 @@
 def groups_of(refs):
     size = len(refs) // STEPS
     return [(step, refs[step * size : (step + 1) * size]) for step in range(STEPS)]
-
-
-def start_all(pairs, sem_ref, first=0):
-    copies = [
-        pltpu.make_async_copy(source, target, sem_ref.at[first + number])
-        for number, (source, target) in enumerate(pairs)
-    ]
-    for copy in copies:
-        copy.start()
-    return copies
 
 
 def add_to(acc_ref, out_ref, step, index, value):
@@ -195,12 +185,11 @@
 
 
 def outer_kernel(rows, *refs):
-    layers = (len(refs) - 8) // 3
+    layers = (len(refs) - 6) // 3
     messages, n_ref = pieces(refs[:layers], refs[layers : 2 * layers]), refs[2 * layers]
-    gifts, rest = refs[2 * layers + 1 : -7], refs[-7:]
-    out_ref, acc_ref, held_ref, p_ref, x_ref, left_ref, sem_ref = rest
+    gifts, rest = refs[2 * layers + 1 : -5], refs[-5:]
+    out_ref, acc_ref, p_ref, x_ref, left_ref = rest
     gifts = pieces(gifts, gifts)
-    copies = []
     hid = acc_ref.shape[1]
     parts = [whole(n_ref, index) for index in range(3)]
     for index in range(4):
@@ -212,13 +201,10 @@
             p_ref[index] = mm(parts[index], operand, (1, 1))
         forward_halves(p_ref, x_ref, None)
         stacked = x_ref[0:4].reshape(4 * hid, x_ref.shape[2])
-        held = [held_ref.at[step * len(back) + slot] for slot in range(len(back))]
+        held = back
         give(held, mm(left_ref[...], stacked), 0, rows)
-        copies += start_all(list(zip(held, back)), sem_ref, step * len(back))
         for index, operand in enumerate((q, q, g)):
             put(index, mm(x_ref[2 * index], operand) + mm(x_ref[2 * index + 1], operand))
-    for copy in copies:
-        copy.wait()
 
 
 def second_halves(act_ref, p_ref, x_ref, r):
@@ -248,16 +234,14 @@
 
 
 def second_kernel(rows, *refs):
-    layers = (len(refs) - 14) // 3
+    layers = (len(refs) - 10) // 3
     sources = pieces(refs[:layers], refs[layers : 2 * layers])
     wh_ref, wl_ref, c_ref = refs[2 * layers : 2 * layers + 3]
-    gifts, rest = refs[2 * layers + 3 : -11], refs[-11:]
+    gifts, rest = refs[2 * layers + 3 : -7], refs[-7:]
     gifts = pieces(gifts, gifts)
-    out_ref, acc_ref, message_ref, act_ref, held_ref, p_ref, x_ref = rest[:7]
-    key_left, value_left, message_sem, held_sem = rest[7:]
-    messages = [message_ref.at[slot] for slot in range(len(sources))]
-    loads = start_all(list(zip(sources, messages)), message_sem)
-    copies = []
+    out_ref, acc_ref, act_ref, p_ref, x_ref = rest[:5]
+    key_left, value_left = rest[5:]
+    messages = sources
     hid = acc_ref.shape[1]
     parts = [whole(c_ref, index) for index in range(3)]
     gate, up, down = [part.T for part in parts]
@@ -270,8 +254,6 @@
             left_ref[:, index * hid : (index + 1) * hid] = item
     for (step, group), (_, back) in zip(groups_of(messages), groups_of(gifts)):
         put = functools.partial(add_to, acc_ref, out_ref, step)
-        for load in loads[step * len(group) : (step + 1) * len(group)]:
-            load.wait()
         k, v = rows_of(group, 0, rows), rows_of(group, rows, rows)
         for index, operand in enumerate((k, k, v)):
             p_ref[index] = mm(parts[index], operand, (1, 1))
@@ -283,16 +265,13 @@
 
         dk = mm(key_left[:, : 8 * hid], stacked(0, 8)) + mm(key_left[:, 8 * hid :], stacked(6, 8))
         dv = mm(value_left[:, : 4 * hid], stacked(8, 12)) + mm(value_left[:, 4 * hid :], x_ref[11])
-        held = [held_ref.at[step * len(back) + slot] for slot in range(len(back))]
+        held = back
         give(held, dk, 0, rows)
         give(held, dv, rows, rows)
         for slot, ref in enumerate(held):
             ref[2 * rows :] = padded_row(d_rate[:, slot * rows : (slot + 1) * rows], ref.shape[1])
-        copies += start_all(list(zip(held, back)), held_sem, step * len(back))
         for index, (one, two, operand) in enumerate(((6, 4, k), (7, 5, k), (11, 10, v))):
             put(index, mm(x_ref[one], operand) + mm(x_ref[two], operand))
-    for copy in copies:
-        copy.wait()
 
 
 def total_of(in_ref):
@@ -388,7 +367,6 @@
     group_tokens = heads * rows // STEPS
     products = pltpu.VMEM((3, hid, group_tokens), F32)
     half_terms = pltpu.VMEM((6, hid, group_tokens), BF16)
-    main = pl.BlockSpec(memory_space=pltpu.HBM)
     grad_part = call(
         functools.partial(inner_kernel, rows),
         part_shape,
@@ -410,14 +388,12 @@
         flops=13 * product,
         vmem=60,
         in_specs=[memory] * (heads + 1),
-        out_specs=[main] * layers + [memory],
+        out_specs=[memory] * (layers + 1),
         scratch_shapes=scratch
         + [
-            pltpu.VMEM((heads, rows, width), BF16),
             products,
             half_terms,
             pltpu.VMEM((width, 4 * hid), BF16),
-            pltpu.SemaphoreType.DMA((heads,)),
         ],
     )(*qg, updated)
     given, d_queries = lax.optimization_barrier((scatter(d_part), along(d_queries, -1)))
@@ -434,19 +410,15 @@
         messages_of(2 * rows + PAD) + (part_shape,),
         flops=24 * product,
         vmem=60,
-        in_specs=[main] * heads + [memory] * 3,
-        out_specs=[main] * layers + [memory],
+        in_specs=[memory] * (heads + 3),
+        out_specs=[memory] * (layers + 1),
         scratch_shapes=scratch
         + [
-            pltpu.VMEM((heads, 2 * rows + PAD, width), BF16),
             products,
-            pltpu.VMEM((heads, 2 * rows + PAD, width), BF16),
             products,
             pltpu.VMEM((12, hid, group_tokens), BF16),
             pltpu.VMEM((width, 10 * hid), BF16),
             pltpu.VMEM((width, 5 * hid), BF16),
-            pltpu.SemaphoreType.DMA((heads,)),
-            pltpu.SemaphoreType.DMA((heads,)),
         ],
     )(*kv, w_high, w_low, cotangent)
     d_kv = along(d_kv, -1)

time: 159 us -> 157 us (0.987)
  Pallas kernels: 37 us -> 35.2 us
where the time goes in v3:
time: 157 us
  starting transfers between devices  59.4 us (38%)
  waiting for transfers between devices  49.6 us (32%)
  Pallas kernels  35.2 us (22%)
  local copies, waits for them, and re-layouts  6.56 us (4%)
  other arithmetic  4.74 us (3%)
    all_to_all x5, waiting for transfers between devices, scatter(): return lax.all_to_all(message, 'p', 0, 0, tiled=True)  25 us
    all_to_all x5, starting transfers between devices, scatter(): return lax.all_to_all(message, 'p', 0, 0, tiled=True)  24 us
    ppermute x12, waiting for transfers between devices, along(): lax.ppermute(m, 'z', pair)  21.9 us
    ppermute x12, starting transfers between devices, along(): lax.ppermute(m, 'z', pair)  18.7 us
    pallas_call x1, Pallas kernels, body(): call(functools.partial(second_kernel, rows), messages_of(2 * rows + PAD)...  13.8 us
    ppermute x16, starting transfers between devices, across(): lax.ppermute(message, 'c', [(0, 1), (1, 0)])  13.1 us
    pallas_call x1, Pallas kernels, body(): call(functools.partial(outer_kernel, rows), messages_of(rows) + (part_sha...  7.35 us
    pallas_call x1, Pallas kernels, body(): call(functools.partial(inner_kernel, rows), part_shape, flops=12 * produc...  7.27 us
  transfers between devices with their start and end apart: 34, of which 19 were waited for; matrix products, arithmetic and copies ran while one was open for 4% of the time, Pallas kernels for 1%

profile of v3, /device:TPU:1, one launch (start us, length us, event | category | flops | bytes accessed | tf_op | source)
XLA Modules:
  0.0 156.6 jit_solution(5558653393252040363)
XLA Ops:
  4.2 4.5 %collective-permute-start = (bf16[544,256]{1,0:T(8,128)(2,1)S(1)}, bf16[544,256]{1,0:T(8,128)(2,1)S(1)}, u32[]{:S(2)}, u32[]{:S(2)}) collective-permute-start(bf16[544,256]{1,0:T(8,128)(2,1)S(1)} %get-tuple-element.50), channel_id=1, source_target_pairs={{0,64},{32,96},{64,0},{96,32},{1,65},{33,97},{65,1},{97,33},{2,66}... | collective-permute-start | bytes 835592 | tf_op jit(solution)/shard_map/ppermute | solution.py:332
  12.9 2.2 %collective-permute-done.refs_1_ = bf16[544,256]{1,0:T(8,128)(2,1)S(1)} collective-permute-done((bf16[544,256]{1,0:T(8,128)(2,1)S(1)}, bf16[544,256]{1,0:T(8,128)(2,1)S(1)}, u32[]{:S(2)}, u32[]{:S(2)}) %collective-permute-start) | collective-permute-done | bytes 278560 | tf_op jit(solution)/shard_map/ppermute | solution.py:332
  15.2 2.1 %collective-permute-start.4 = (bf16[544,256]{1,0:T(8,128)(2,1)S(1)}, bf16[544,256]{1,0:T(8,128)(2,1)S(1)}, u32[]{:S(2)}, u32[]{:S(2)}) collective-permute-start(bf16[544,256]{1,0:T(8,128)(2,1)S(1)} %collective-permute-done.refs_1_), channel_id=1, source_target_pairs={{0,1},{1,0},{2,3},{3,2},{4,5},{5,4},{6,7},{7,6},{8,9},{9,8},{10,11... | collective-permute-start | bytes 835592 | tf_op jit(solution)/shard_map/ppermute | solution.py:336
  17.2 4.6 %collective-permute-done.1.refs_2_ = bf16[544,256]{1,0:T(8,128)(2,1)S(1)} collective-permute-done((bf16[544,256]{1,0:T(8,128)(2,1)S(1)}, bf16[544,256]{1,0:T(8,128)(2,1)S(1)}, u32[]{:S(2)}, u32[]{:S(2)}) %collective-permute-start.1) | collective-permute-done | bytes 278560 | tf_op jit(solution)/shard_map/ppermute | solution.py:332
  23.1 3.1 %fusion = (bf16[3,512,256]{2,1,0:T(8,128)(2,1)}, f32[3,512,256]{2,1,0:T(8,128)}) fusion(f32[2,3,512,256]{3,2,1,0:T(8,128)} %param.10, s32[]{:T(128)S(6)} %select_n.81), kind=kLoop, calls=%fused_computation.2 | loop fusion | flops 1179648 | bytes 3932164 | tf_op jit(solution)/shard_map/convert_element_type | solution.py:345
  27.2 7.3 %shard_map.103 = bf16[16,3,32,256]{3,2,1,0:T(8,128)(2,1)} custom-call(bf16[544,256]{1,0:T(8,128)(2,1)} %copy-done.7, bf16[544,256]{1,0:T(8,128)(2,1)} %copy-done.12, bf16[544,256]{1,0:T(8,128)(2,1)} %copy-done.13, bf16[544,256]{1,0:T(8,128)(2,1)} %copy-done.14, bf16[544,256]{1,0:T(8,128)(2,1)} %copy-done.15, bf16[544,256]{1,0:T(8,128)(2,1)} %copy-done.16, ...), custom_call_target="tpu_custom_call" | custom-call | flops 3221225472 | bytes 4194304 | tf_op jit(solution)/shard_map/pallas_call | solution.py:370
  34.5 6.9 %all-to-all-start = ((bf16[16,96,256]{2,1,0:T(8,128)(2,1)}), bf16[16,96,256]{2,1,0:T(8,128)(2,1)S(1)}, u32[]{:S(2)}, u32[]{:S(2)}) async-start(bf16[16,96,256]{2,1,0:T(8,128)(2,1)} %bitcast.40), calls=%async_computation | async-start | bytes 1572864 | tf_op jit(solution)/shard_map/all_to_all | solution.py:340
  45.0 6.3 %collective-permute-done.7.refs_1_ = bf16[512,256]{1,0:T(8,128)(2,1)S(1)} collective-permute-done((bf16[512,256]{1,0:T(8,128)(2,1)S(1)}, bf16[512,256]{1,0:T(8,128)(2,1)S(1)}, u32[]{:S(2)}, u32[]{:S(2)}) %collective-permute-start.7) | collective-permute-done | bytes 262176 | tf_op jit(solution)/shard_map/ppermute | solution.py:332
  51.3 4.0 %all-to-all-done.in_ref = bf16[16,96,256]{2,1,0:T(8,128)(2,1)S(1)} async-done(((bf16[16,96,256]{2,1,0:T(8,128)(2,1)}), bf16[16,96,256]{2,1,0:T(8,128)(2,1)S(1)}, u32[]{:S(2)}, u32[]{:S(2)}) %all-to-all-start) | async-done | bytes 786464 | tf_op jit(solution)/shard_map/all_to_all | solution.py:340
  56.4 3.7 %all-to-all-start.1 = ((bf16[16,96,256]{2,1,0:T(8,128)(2,1)}), bf16[16,96,256]{2,1,0:T(8,128)(2,1)S(1)}, u32[]{:S(2)}, u32[]{:S(2)}) async-start(bf16[16,96,256]{2,1,0:T(8,128)(2,1)} %get-tuple-element.59), calls=%async_computation.1 | async-start | bytes 1572864 | tf_op jit(solution)/shard_map/all_to_all | solution.py:340
  60.6 2.2 %collective-permute-start.9 = (bf16[512,256]{1,0:T(8,128)(2,1)S(1)}, bf16[512,256]{1,0:T(8,128)(2,1)S(1)}, u32[]{:S(2)}, u32[]{:S(2)}) collective-permute-start(bf16[512,256]{1,0:T(8,128)(2,1)S(1)} %get-tuple-element.57), channel_id=1, source_target_pairs={{0,96},{32,0},{64,32},{96,64},{1,97},{33,1},{65,33},{97,65},{2,98}... | collective-permute-start | bytes 786440 | tf_op jit(solution)/shard_map/ppermute | solution.py:332
  64.8 3.0 %collective-permute-done.8.refs_2_ = bf16[512,256]{1,0:T(8,128)(2,1)S(1)} collective-permute-done((bf16[512,256]{1,0:T(8,128)(2,1)S(1)}, bf16[512,256]{1,0:T(8,128)(2,1)S(1)}, u32[]{:S(2)}, u32[]{:S(2)}) %collective-permute-start.8) | collective-permute-done | bytes 262176 | tf_op jit(solution)/shard_map/ppermute | solution.py:332
  67.7 2.3 %collective-permute-start.12 = (bf16[512,256]{1,0:T(8,128)(2,1)S(1)}, bf16[512,256]{1,0:T(8,128)(2,1)S(1)}, u32[]{:S(2)}, u32[]{:S(2)}) collective-permute-start(bf16[512,256]{1,0:T(8,128)(2,1)S(1)} %collective-permute-done.8.refs_2_), channel_id=1, source_target_pairs={{0,1},{1,0},{2,3},{3,2},{4,5},{5,4},{6,7},{7,6},{8,9},{9,8},{10,11... | collective-permute-start | bytes 786440 | tf_op jit(solution)/shard_map/ppermute | solution.py:336
  73.7 7.3 %shard_map.105 = (bf16[256,256]{1,0:T(8,128)(2,1)}, bf16[256,256]{1,0:T(8,128)(2,1)}, bf16[256,256]{1,0:T(8,128)(2,1)}, bf16[256,256]{1,0:T(8,128)(2,1)}, bf16[16,3,32,256]{3,2,1,0:T(8,128)(2,1)}) custom-call(bf16[512,256]{1,0:T(8,128)(2,1)} %copy-done.8, bf16[512,256]{1,0:T(8,128)(2,1)} %copy-done.22, bf16[512,256]{1,0:T(8,128)(2,1)} %copy-done.23, ...), custom_call_target="tpu_custom_call" | custom-call | flops 3489660928 | bytes 4194304 | tf_op jit(solution)/shard_map/pallas_call | solution.py:385
  81.1 6.0 %all-to-all-start.2 = ((bf16[16,96,256]{2,1,0:T(8,128)(2,1)}), bf16[16,96,256]{2,1,0:T(8,128)(2,1)S(1)}, u32[]{:S(2)}, u32[]{:S(2)}) async-start(bf16[16,96,256]{2,1,0:T(8,128)(2,1)} %bitcast.42), calls=%async_computation.2 | async-start | bytes 1572864 | tf_op jit(solution)/shard_map/all_to_all | solution.py:340
  90.5 2.6 %collective-permute-done.14.refs_1_ = bf16[256,256]{1,0:T(8,128)(2,1)S(1)} collective-permute-done((bf16[256,256]{1,0:T(8,128)(2,1)S(1)}, bf16[256,256]{1,0:T(8,128)(2,1)S(1)}, u32[]{:S(2)}, u32[]{:S(2)}) %collective-permute-start.14) | collective-permute-done | bytes 131104 | tf_op jit(solution)/shard_map/ppermute | solution.py:332
  93.1 2.8 %collective-permute-done.15.refs_2_ = bf16[256,256]{1,0:T(8,128)(2,1)S(1)} collective-permute-done((bf16[256,256]{1,0:T(8,128)(2,1)S(1)}, bf16[256,256]{1,0:T(8,128)(2,1)S(1)}, u32[]{:S(2)}, u32[]{:S(2)}) %collective-permute-start.15) | collective-permute-done | bytes 131104 | tf_op jit(solution)/shard_map/ppermute | solution.py:332
  96.3 4.3 %all-to-all-done.2.in_ref = bf16[16,96,256]{2,1,0:T(8,128)(2,1)S(1)} async-done(((bf16[16,96,256]{2,1,0:T(8,128)(2,1)}), bf16[16,96,256]{2,1,0:T(8,128)(2,1)S(1)}, u32[]{:S(2)}, u32[]{:S(2)}) %all-to-all-start.2) | async-done | bytes 786464 | tf_op jit(solution)/shard_map/all_to_all | solution.py:340
  101.7 3.6 %all-to-all-start.3 = ((bf16[16,96,256]{2,1,0:T(8,128)(2,1)}), bf16[16,96,256]{2,1,0:T(8,128)(2,1)S(1)}, u32[]{:S(2)}, u32[]{:S(2)}) async-start(bf16[16,96,256]{2,1,0:T(8,128)(2,1)} %get-tuple-element.72), calls=%async_computation.3 | async-start | bytes 1572864 | tf_op jit(solution)/shard_map/all_to_all | solution.py:340
  110.5 7.6 %all-to-all-done.3 = bf16[16,96,256]{2,1,0:T(8,128)(2,1)S(1)} async-done(((bf16[16,96,256]{2,1,0:T(8,128)(2,1)}), bf16[16,96,256]{2,1,0:T(8,128)(2,1)S(1)}, u32[]{:S(2)}, u32[]{:S(2)}) %all-to-all-start.3) | async-done | bytes 786464 | tf_op jit(solution)/shard_map/all_to_all | solution.py:340
  119.0 13.8 %shard_map.108 = (bf16[544,256]{1,0:T(8,128)(2,1)}, bf16[544,256]{1,0:T(8,128)(2,1)}, bf16[544,256]{1,0:T(8,128)(2,1)}, bf16[544,256]{1,0:T(8,128)(2,1)}, bf16[16,3,32,256]{3,2,1,0:T(8,128)(2,1)}) custom-call(bf16[544,256]{1,0:T(8,128)(2,1)} %copy-done.7, bf16[544,256]{1,0:T(8,128)(2,1)} %copy-done.12, bf16[544,256]{1,0:T(8,128)(2,1)} %copy-done.13, ...), custom_call_target="tpu_custom_call" | custom-call | flops 6442450944 | bytes 4194304 | tf_op jit(solution)/shard_map/pallas_call | solution.py:408
  132.8 3.8 %all-to-all-start.4 = ((bf16[16,96,256]{2,1,0:T(8,128)(2,1)}), bf16[16,96,256]{2,1,0:T(8,128)(2,1)S(1)}, u32[]{:S(2)}, u32[]{:S(2)}) async-start(bf16[16,96,256]{2,1,0:T(8,128)(2,1)} %bitcast.41), calls=%async_computation.4 | async-start | bytes 1572864 | tf_op jit(solution)/shard_map/all_to_all | solution.py:340
  140.0 8.4 %all-to-all-done.4.in_ref = bf16[16,96,256]{2,1,0:T(8,128)(2,1)S(1)} async-done(((bf16[16,96,256]{2,1,0:T(8,128)(2,1)}), bf16[16,96,256]{2,1,0:T(8,128)(2,1)S(1)}, u32[]{:S(2)}, u32[]{:S(2)}) %all-to-all-start.4) | async-done | bytes 786464 | tf_op jit(solution)/shard_map/all_to_all | solution.py:340
  148.5 3.7 %collective-permute-start.28 = (f32[3,16,256]{2,1,0:T(8,128)S(1)}, f32[3,16,256]{2,1,0:T(8,128)S(1)}, u32[]{:S(2)}, u32[]{:S(2)}) collective-permute-start(f32[3,16,256]{2,1,0:T(8,128)S(1)} %dynamic-slice_bitcast_fusion.1), channel_id=1, source_target_pairs={{0,1},{1,0},{2,3},{3,2},{4,5},{5,4},{6,7},{7,6},{8,9},{9,8},{10,11... | collective-permute-start | bytes 147464 | tf_op jit(solution)/shard_map/ppermute | solution.py:429
  (125 shorter events, 39.6 us)
Async XLA Ops:
  4.2 10.9 %collective-permute-start = (bf16[544,256]{1,0:T(8,128)(2,1)S(1)}, bf16[544,256]{1,0:T(8,128)(2,1)S(1)}, u32[]{:S(2)}, u32[]{:S(2)}) collective-permute-start(bf16[544,256]{1,0:T(8,128)(2,1)S(1)} %get-tuple-element.50), channel_id=1, source_target_pairs={{0,64},{32,96},{64,0},{96,32},{1,65},{33,97},{65,1},{97,33},{2,66}... | collective-permute-start | bytes 835592 | tf_op jit(solution)/shard_map/ppermute | solution.py:332
  8.8 13.1 %collective-permute-start.1 = (bf16[544,256]{1,0:T(8,128)(2,1)S(1)}, bf16[544,256]{1,0:T(8,128)(2,1)S(1)}, u32[]{:S(2)}, u32[]{:S(2)}) collective-permute-start(bf16[544,256]{1,0:T(8,128)(2,1)S(1)} %get-tuple-element.51), channel_id=1, source_target_pairs={{0,32},{32,64},{64,96},{96,0},{1,33},{33,65},{65,97},{97,1},{2,34}... | collective-permute-start | bytes 835592 | tf_op jit(solution)/shard_map/ppermute | solution.py:332
  9.5 12.8 %collective-permute-start.2 = (bf16[544,256]{1,0:T(8,128)(2,1)S(1)}, bf16[544,256]{1,0:T(8,128)(2,1)S(1)}, u32[]{:S(2)}, u32[]{:S(2)}) collective-permute-start(bf16[544,256]{1,0:T(8,128)(2,1)S(1)} %get-tuple-element.52), channel_id=1, source_target_pairs={{0,96},{32,0},{64,32},{96,64},{1,97},{33,1},{65,33},{97,65},{2,98}... | collective-permute-start | bytes 835592 | tf_op jit(solution)/shard_map/ppermute | solution.py:332
  11.4 14.8 %collective-permute-start.3 = (bf16[544,256]{1,0:T(8,128)(2,1)S(1)}, bf16[544,256]{1,0:T(8,128)(2,1)S(1)}, u32[]{:S(2)}, u32[]{:S(2)}) collective-permute-start(bf16[544,256]{1,0:T(8,128)(2,1)S(1)} %get-tuple-element.49.refs_0_), channel_id=1, source_target_pairs={{0,1},{1,0},{2,3},{3,2},{4,5},{5,4},{6,7},{7,6},{8,9},{9,8},{10,11... | collective-permute-start | bytes 835592 | tf_op jit(solution)/shard_map/ppermute | solution.py:336
  15.2 11.0 %collective-permute-start.4 = (bf16[544,256]{1,0:T(8,128)(2,1)S(1)}, bf16[544,256]{1,0:T(8,128)(2,1)S(1)}, u32[]{:S(2)}, u32[]{:S(2)}) collective-permute-start(bf16[544,256]{1,0:T(8,128)(2,1)S(1)} %collective-permute-done.refs_1_), channel_id=1, source_target_pairs={{0,1},{1,0},{2,3},{3,2},{4,5},{5,4},{6,7},{7,6},{8,9},{9,8},{10,11... | collective-permute-start | bytes 835592 | tf_op jit(solution)/shard_map/ppermute | solution.py:336
  21.8 4.4 %collective-permute-start.5 = (bf16[544,256]{1,0:T(8,128)(2,1)S(1)}, bf16[544,256]{1,0:T(8,128)(2,1)S(1)}, u32[]{:S(2)}, u32[]{:S(2)}) collective-permute-start(bf16[544,256]{1,0:T(8,128)(2,1)S(1)} %collective-permute-done.1.refs_2_), channel_id=1, source_target_pairs={{0,1},{1,0},{2,3},{3,2},{4,5},{5,4},{6,7},{7,6},{8,9},{9,8},{10,11... | collective-permute-start | bytes 835592 | tf_op jit(solution)/shard_map/ppermute | solution.py:336
  22.3 3.9 %collective-permute-start.6 = (bf16[544,256]{1,0:T(8,128)(2,1)S(1)}, bf16[544,256]{1,0:T(8,128)(2,1)S(1)}, u32[]{:S(2)}, u32[]{:S(2)}) collective-permute-start(bf16[544,256]{1,0:T(8,128)(2,1)S(1)} %collective-permute-done.2.refs_3_), channel_id=1, source_target_pairs={{0,1},{1,0},{2,3},{3,2},{4,5},{5,4},{6,7},{7,6},{8,9},{9,8},{10,11... | collective-permute-start | bytes 835592 | tf_op jit(solution)/shard_map/ppermute | solution.py:336
  34.5 20.7 %all-to-all-start = ((bf16[16,96,256]{2,1,0:T(8,128)(2,1)}), bf16[16,96,256]{2,1,0:T(8,128)(2,1)S(1)}, u32[]{:S(2)}, u32[]{:S(2)}) async-start(bf16[16,96,256]{2,1,0:T(8,128)(2,1)} %bitcast.40), calls=%async_computation | async-start | bytes 1572864 | tf_op jit(solution)/shard_map/all_to_all | solution.py:340
  42.2 9.1 %collective-permute-start.7 = (bf16[512,256]{1,0:T(8,128)(2,1)S(1)}, bf16[512,256]{1,0:T(8,128)(2,1)S(1)}, u32[]{:S(2)}, u32[]{:S(2)}) collective-permute-start(bf16[512,256]{1,0:T(8,128)(2,1)S(1)} %get-tuple-element.54), channel_id=1, source_target_pairs={{0,64},{32,96},{64,0},{96,32},{1,65},{33,97},{65,1},{97,33},{2,66}... | collective-permute-start | bytes 786440 | tf_op jit(solution)/shard_map/ppermute | solution.py:332
  56.4 16.5 %all-to-all-start.1 = ((bf16[16,96,256]{2,1,0:T(8,128)(2,1)}), bf16[16,96,256]{2,1,0:T(8,128)(2,1)S(1)}, u32[]{:S(2)}, u32[]{:S(2)}) async-start(bf16[16,96,256]{2,1,0:T(8,128)(2,1)} %get-tuple-element.59), calls=%async_computation.1 | async-start | bytes 1572864 | tf_op jit(solution)/shard_map/all_to_all | solution.py:340
  60.1 7.7 %collective-permute-start.8 = (bf16[512,256]{1,0:T(8,128)(2,1)S(1)}, bf16[512,256]{1,0:T(8,128)(2,1)S(1)}, u32[]{:S(2)}, u32[]{:S(2)}) collective-permute-start(bf16[512,256]{1,0:T(8,128)(2,1)S(1)} %get-tuple-element.56), channel_id=1, source_target_pairs={{0,32},{32,64},{64,96},{96,0},{1,33},{33,65},{65,97},{97,1},{2,34}... | collective-permute-start | bytes 786440 | tf_op jit(solution)/shard_map/ppermute | solution.py:332
  60.6 9.5 %collective-permute-start.9 = (bf16[512,256]{1,0:T(8,128)(2,1)S(1)}, bf16[512,256]{1,0:T(8,128)(2,1)S(1)}, u32[]{:S(2)}, u32[]{:S(2)}) collective-permute-start(bf16[512,256]{1,0:T(8,128)(2,1)S(1)} %get-tuple-element.57), channel_id=1, source_target_pairs={{0,96},{32,0},{64,32},{96,64},{1,97},{33,1},{65,33},{97,65},{2,98}... | collective-permute-start | bytes 786440 | tf_op jit(solution)/shard_map/ppermute | solution.py:332
  62.8 7.8 %collective-permute-start.10 = (bf16[512,256]{1,0:T(8,128)(2,1)S(1)}, bf16[512,256]{1,0:T(8,128)(2,1)S(1)}, u32[]{:S(2)}, u32[]{:S(2)}) collective-permute-start(bf16[512,256]{1,0:T(8,128)(2,1)S(1)} %get-tuple-element.53.refs_0_), channel_id=1, source_target_pairs={{0,1},{1,0},{2,3},{3,2},{4,5},{5,4},{6,7},{7,6},{8,9},{9,8},{10,11... | collective-permute-start | bytes 786440 | tf_op jit(solution)/shard_map/ppermute | solution.py:336
  67.7 3.5 %collective-permute-start.12 = (bf16[512,256]{1,0:T(8,128)(2,1)S(1)}, bf16[512,256]{1,0:T(8,128)(2,1)S(1)}, u32[]{:S(2)}, u32[]{:S(2)}) collective-permute-start(bf16[512,256]{1,0:T(8,128)(2,1)S(1)} %collective-permute-done.8.refs_2_), channel_id=1, source_target_pairs={{0,1},{1,0},{2,3},{3,2},{4,5},{5,4},{6,7},{7,6},{8,9},{9,8},{10,11... | collective-permute-start | bytes 786440 | tf_op jit(solution)/shard_map/ppermute | solution.py:336
  81.1 19.5 %all-to-all-start.2 = ((bf16[16,96,256]{2,1,0:T(8,128)(2,1)}), bf16[16,96,256]{2,1,0:T(8,128)(2,1)S(1)}, u32[]{:S(2)}, u32[]{:S(2)}) async-start(bf16[16,96,256]{2,1,0:T(8,128)(2,1)} %bitcast.42), calls=%async_computation.2 | async-start | bytes 1572864 | tf_op jit(solution)/shard_map/all_to_all | solution.py:340
  87.1 6.0 %collective-permute-start.14 = (bf16[256,256]{1,0:T(8,128)(2,1)S(1)}, bf16[256,256]{1,0:T(8,128)(2,1)S(1)}, u32[]{:S(2)}, u32[]{:S(2)}) collective-permute-start(bf16[256,256]{1,0:T(8,128)(2,1)S(1)} %copy-done.31), channel_id=1, source_target_pairs={{0,64},{32,96},{64,0},{96,32},{1,65},{33,97},{65,1},{97,33},{2,66}... | collective-permute-start | bytes 393224 | tf_op jit(solution)/shard_map/ppermute | solution.py:332
  89.0 6.8 %collective-permute-start.15 = (bf16[256,256]{1,0:T(8,128)(2,1)S(1)}, bf16[256,256]{1,0:T(8,128)(2,1)S(1)}, u32[]{:S(2)}, u32[]{:S(2)}) collective-permute-start(bf16[256,256]{1,0:T(8,128)(2,1)S(1)} %copy-done.30), channel_id=1, source_target_pairs={{0,96},{32,0},{64,32},{96,64},{1,97},{33,1},{65,33},{97,65},{2,98}... | collective-permute-start | bytes 393224 | tf_op jit(solution)/shard_map/ppermute | solution.py:332
  89.7 6.7 %collective-permute-start.16 = (bf16[256,256]{1,0:T(8,128)(2,1)S(1)}, bf16[256,256]{1,0:T(8,128)(2,1)S(1)}, u32[]{:S(2)}, u32[]{:S(2)}) collective-permute-start(bf16[256,256]{1,0:T(8,128)(2,1)S(1)} %copy-done.29), channel_id=1, source_target_pairs={{0,32},{32,64},{64,96},{96,0},{1,33},{33,65},{65,97},{97,1},{2,34}... | collective-permute-start | bytes 393224 | tf_op jit(solution)/shard_map/ppermute | solution.py:332
  101.7 16.3 %all-to-all-start.3 = ((bf16[16,96,256]{2,1,0:T(8,128)(2,1)}), bf16[16,96,256]{2,1,0:T(8,128)(2,1)S(1)}, u32[]{:S(2)}, u32[]{:S(2)}) async-start(bf16[16,96,256]{2,1,0:T(8,128)(2,1)} %get-tuple-element.72), calls=%async_computation.3 | async-start | bytes 1572864 | tf_op jit(solution)/shard_map/all_to_all | solution.py:340
  132.8 15.5 %all-to-all-start.4 = ((bf16[16,96,256]{2,1,0:T(8,128)(2,1)}), bf16[16,96,256]{2,1,0:T(8,128)(2,1)S(1)}, u32[]{:S(2)}, u32[]{:S(2)}) async-start(bf16[16,96,256]{2,1,0:T(8,128)(2,1)} %bitcast.41), calls=%async_computation.4 | async-start | bytes 1572864 | tf_op jit(solution)/shard_map/all_to_all | solution.py:340
  136.6 15.7 %collective-permute-start.22 = (bf16[544,256]{1,0:T(8,128)(2,1)S(1)}, bf16[544,256]{1,0:T(8,128)(2,1)S(1)}, u32[]{:S(2)}, u32[]{:S(2)}) collective-permute-start(bf16[544,256]{1,0:T(8,128)(2,1)S(1)} %copy-done.21), channel_id=1, source_target_pairs={{0,64},{32,96},{64,0},{96,32},{1,65},{33,97},{65,1},{97,33},{2,66}... | collective-permute-start | bytes 835592 | tf_op jit(solution)/shard_map/ppermute | solution.py:332
  138.5 14.1 %collective-permute-start.24 = (bf16[544,256]{1,0:T(8,128)(2,1)S(1)}, bf16[544,256]{1,0:T(8,128)(2,1)S(1)}, u32[]{:S(2)}, u32[]{:S(2)}) collective-permute-start(bf16[544,256]{1,0:T(8,128)(2,1)S(1)} %copy-done.20), channel_id=1, source_target_pairs={{0,96},{32,0},{64,32},{96,64},{1,97},{33,1},{65,33},{97,65},{2,98}... | collective-permute-start | bytes 835592 | tf_op jit(solution)/shard_map/ppermute | solution.py:332
  139.1 14.1 %collective-permute-start.26 = (bf16[544,256]{1,0:T(8,128)(2,1)S(1)}, bf16[544,256]{1,0:T(8,128)(2,1)S(1)}, u32[]{:S(2)}, u32[]{:S(2)}) collective-permute-start(bf16[544,256]{1,0:T(8,128)(2,1)S(1)} %copy-done.19), channel_id=1, source_target_pairs={{0,32},{32,64},{64,96},{96,0},{1,33},{33,65},{65,97},{97,1},{2,34}... | collective-permute-start | bytes 835592 | tf_op jit(solution)/shard_map/ppermute | solution.py:332
  148.5 4.7 %collective-permute-start.28 = (f32[3,16,256]{2,1,0:T(8,128)S(1)}, f32[3,16,256]{2,1,0:T(8,128)S(1)}, u32[]{:S(2)}, u32[]{:S(2)}) collective-permute-start(f32[3,16,256]{2,1,0:T(8,128)S(1)} %dynamic-slice_bitcast_fusion.1), channel_id=1, source_target_pairs={{0,1},{1,0},{2,3},{3,2},{4,5},{5,4},{6,7},{7,6},{8,9},{9,8},{10,11... | collective-permute-start | bytes 147464 | tf_op jit(solution)/shard_map/ppermute | solution.py:429
  (42 other events, 244.3 us)

commit v4 on v3

--- a/solution.py
+++ b/solution.py
@@ -12,7 +12,7 @@
 PAD = 16
 STEPS = 2
 ROW_BLOCK = 16
-COLUMN_BLOCK = 256
+COLUMN_BLOCK = 512
 F32 = jnp.float32
 BF16 = jnp.bfloat16
 
@@ -371,7 +371,7 @@
         functools.partial(inner_kernel, rows),
         part_shape,
         flops=12 * product,
-        vmem=60,
+        vmem=54,
         in_specs=[memory] * (heads + 1),
         out_specs=memory,
         scratch_shapes=scratch + [products, half_terms] + [pltpu.VMEM((3, hid, width), BF16)] * 2,
@@ -386,7 +386,7 @@
         functools.partial(outer_kernel, rows),
         messages_of(rows) + (part_shape,),
         flops=13 * product,
-        vmem=60,
+        vmem=54,
         in_specs=[memory] * (heads + 1),
         out_specs=[memory] * (layers + 1),
         scratch_shapes=scratch
@@ -409,7 +409,7 @@
         functools.partial(second_kernel, rows),
         messages_of(2 * rows + PAD) + (part_shape,),
         flops=24 * product,
-        vmem=60,
+        vmem=54,
         in_specs=[memory] * (heads + 3),
         out_specs=[memory] * (layers + 1),
         scratch_shapes=scratch

time: 157 us -> 157 us (level)
  no operation moved by 1% of the time
where the time goes in v4:
time: 157 us
  starting transfers between devices  59.4 us (38%)
  waiting for transfers between devices  49.6 us (32%)
  Pallas kernels  35.2 us (22%)
  local copies, waits for them, and re-layouts  6.56 us (4%)
  other arithmetic  4.74 us (3%)
    all_to_all x5, waiting for transfers between devices, scatter(): return lax.all_to_all(message, 'p', 0, 0, tiled=True)  25 us
    all_to_all x5, starting transfers between devices, scatter(): return lax.all_to_all(message, 'p', 0, 0, tiled=True)  24 us
    ppermute x12, waiting for transfers between devices, along(): lax.ppermute(m, 'z', pair)  21.9 us
    ppermute x12, starting transfers between devices, along(): lax.ppermute(m, 'z', pair)  18.7 us
    pallas_call x1, Pallas kernels, body(): call(functools.partial(second_kernel, rows), messages_of(2 * rows + PAD)...  13.8 us
    ppermute x16, starting transfers between devices, across(): lax.ppermute(message, 'c', [(0, 1), (1, 0)])  13.1 us
    pallas_call x1, Pallas kernels, body(): call(functools.partial(outer_kernel, rows), messages_of(rows) + (part_sha...  7.35 us
    pallas_call x1, Pallas kernels, body(): call(functools.partial(inner_kernel, rows), part_shape, flops=12 * produc...  7.27 us
  transfers between devices with their start and end apart: 34, of which 19 were waited for; matrix products, arithmetic and copies ran while one was open for 4% of the time, Pallas kernels for 1%

profile of v4, /device:TPU:1, one launch (start us, length us, event | category | flops | bytes accessed | tf_op | source)
XLA Modules:
  0.0 156.6 jit_solution(14920966009733512183)
XLA Ops:
  4.2 4.5 %collective-permute-start = (bf16[544,256]{1,0:T(8,128)(2,1)S(1)}, bf16[544,256]{1,0:T(8,128)(2,1)S(1)}, u32[]{:S(2)}, u32[]{:S(2)}) collective-permute-start(bf16[544,256]{1,0:T(8,128)(2,1)S(1)} %get-tuple-element.50), channel_id=1, source_target_pairs={{0,64},{32,96},{64,0},{96,32},{1,65},{33,97},{65,1},{97,33},{2,66}... | collective-permute-start | bytes 835592 | tf_op jit(solution)/shard_map/ppermute | solution.py:332
  12.9 2.2 %collective-permute-done.refs_1_ = bf16[544,256]{1,0:T(8,128)(2,1)S(1)} collective-permute-done((bf16[544,256]{1,0:T(8,128)(2,1)S(1)}, bf16[544,256]{1,0:T(8,128)(2,1)S(1)}, u32[]{:S(2)}, u32[]{:S(2)}) %collective-permute-start) | collective-permute-done | bytes 278560 | tf_op jit(solution)/shard_map/ppermute | solution.py:332
  15.2 2.1 %collective-permute-start.4 = (bf16[544,256]{1,0:T(8,128)(2,1)S(1)}, bf16[544,256]{1,0:T(8,128)(2,1)S(1)}, u32[]{:S(2)}, u32[]{:S(2)}) collective-permute-start(bf16[544,256]{1,0:T(8,128)(2,1)S(1)} %collective-permute-done.refs_1_), channel_id=1, source_target_pairs={{0,1},{1,0},{2,3},{3,2},{4,5},{5,4},{6,7},{7,6},{8,9},{9,8},{10,11... | collective-permute-start | bytes 835592 | tf_op jit(solution)/shard_map/ppermute | solution.py:336
  17.2 4.6 %collective-permute-done.1.refs_2_ = bf16[544,256]{1,0:T(8,128)(2,1)S(1)} collective-permute-done((bf16[544,256]{1,0:T(8,128)(2,1)S(1)}, bf16[544,256]{1,0:T(8,128)(2,1)S(1)}, u32[]{:S(2)}, u32[]{:S(2)}) %collective-permute-start.1) | collective-permute-done | bytes 278560 | tf_op jit(solution)/shard_map/ppermute | solution.py:332
  23.1 3.1 %fusion = (bf16[3,512,256]{2,1,0:T(8,128)(2,1)}, f32[3,512,256]{2,1,0:T(8,128)}) fusion(f32[2,3,512,256]{3,2,1,0:T(8,128)} %param.10, s32[]{:T(128)S(6)} %select_n.81), kind=kLoop, calls=%fused_computation.2 | loop fusion | flops 1179648 | bytes 3932164 | tf_op jit(solution)/shard_map/convert_element_type | solution.py:345
  27.2 7.3 %shard_map.103 = bf16[16,3,32,256]{3,2,1,0:T(8,128)(2,1)} custom-call(bf16[544,256]{1,0:T(8,128)(2,1)} %copy-done.7, bf16[544,256]{1,0:T(8,128)(2,1)} %copy-done.12, bf16[544,256]{1,0:T(8,128)(2,1)} %copy-done.13, bf16[544,256]{1,0:T(8,128)(2,1)} %copy-done.14, bf16[544,256]{1,0:T(8,128)(2,1)} %copy-done.15, bf16[544,256]{1,0:T(8,128)(2,1)} %copy-done.16, ...), custom_call_target="tpu_custom_call" | custom-call | flops 3221225472 | bytes 4194304 | tf_op jit(solution)/shard_map/pallas_call | solution.py:370
  34.5 6.9 %all-to-all-start = ((bf16[16,96,256]{2,1,0:T(8,128)(2,1)}), bf16[16,96,256]{2,1,0:T(8,128)(2,1)S(1)}, u32[]{:S(2)}, u32[]{:S(2)}) async-start(bf16[16,96,256]{2,1,0:T(8,128)(2,1)} %bitcast.40), calls=%async_computation | async-start | bytes 1572864 | tf_op jit(solution)/shard_map/all_to_all | solution.py:340
  45.0 6.3 %collective-permute-done.7.refs_1_ = bf16[512,256]{1,0:T(8,128)(2,1)S(1)} collective-permute-done((bf16[512,256]{1,0:T(8,128)(2,1)S(1)}, bf16[512,256]{1,0:T(8,128)(2,1)S(1)}, u32[]{:S(2)}, u32[]{:S(2)}) %collective-permute-start.7) | collective-permute-done | bytes 262176 | tf_op jit(solution)/shard_map/ppermute | solution.py:332
  51.3 4.0 %all-to-all-done.in_ref = bf16[16,96,256]{2,1,0:T(8,128)(2,1)S(1)} async-done(((bf16[16,96,256]{2,1,0:T(8,128)(2,1)}), bf16[16,96,256]{2,1,0:T(8,128)(2,1)S(1)}, u32[]{:S(2)}, u32[]{:S(2)}) %all-to-all-start) | async-done | bytes 786464 | tf_op jit(solution)/shard_map/all_to_all | solution.py:340
  56.4 3.7 %all-to-all-start.1 = ((bf16[16,96,256]{2,1,0:T(8,128)(2,1)}), bf16[16,96,256]{2,1,0:T(8,128)(2,1)S(1)}, u32[]{:S(2)}, u32[]{:S(2)}) async-start(bf16[16,96,256]{2,1,0:T(8,128)(2,1)} %get-tuple-element.59), calls=%async_computation.1 | async-start | bytes 1572864 | tf_op jit(solution)/shard_map/all_to_all | solution.py:340
  60.6 2.2 %collective-permute-start.9 = (bf16[512,256]{1,0:T(8,128)(2,1)S(1)}, bf16[512,256]{1,0:T(8,128)(2,1)S(1)}, u32[]{:S(2)}, u32[]{:S(2)}) collective-permute-start(bf16[512,256]{1,0:T(8,128)(2,1)S(1)} %get-tuple-element.57), channel_id=1, source_target_pairs={{0,96},{32,0},{64,32},{96,64},{1,97},{33,1},{65,33},{97,65},{2,98}... | collective-permute-start | bytes 786440 | tf_op jit(solution)/shard_map/ppermute | solution.py:332
  64.8 3.0 %collective-permute-done.8.refs_2_ = bf16[512,256]{1,0:T(8,128)(2,1)S(1)} collective-permute-done((bf16[512,256]{1,0:T(8,128)(2,1)S(1)}, bf16[512,256]{1,0:T(8,128)(2,1)S(1)}, u32[]{:S(2)}, u32[]{:S(2)}) %collective-permute-start.8) | collective-permute-done | bytes 262176 | tf_op jit(solution)/shard_map/ppermute | solution.py:332
  67.7 2.3 %collective-permute-start.12 = (bf16[512,256]{1,0:T(8,128)(2,1)S(1)}, bf16[512,256]{1,0:T(8,128)(2,1)S(1)}, u32[]{:S(2)}, u32[]{:S(2)}) collective-permute-start(bf16[512,256]{1,0:T(8,128)(2,1)S(1)} %collective-permute-done.8.refs_2_), channel_id=1, source_target_pairs={{0,1},{1,0},{2,3},{3,2},{4,5},{5,4},{6,7},{7,6},{8,9},{9,8},{10,11... | collective-permute-start | bytes 786440 | tf_op jit(solution)/shard_map/ppermute | solution.py:336
  73.7 7.3 %shard_map.105 = (bf16[256,256]{1,0:T(8,128)(2,1)}, bf16[256,256]{1,0:T(8,128)(2,1)}, bf16[256,256]{1,0:T(8,128)(2,1)}, bf16[256,256]{1,0:T(8,128)(2,1)}, bf16[16,3,32,256]{3,2,1,0:T(8,128)(2,1)}) custom-call(bf16[512,256]{1,0:T(8,128)(2,1)} %copy-done.8, bf16[512,256]{1,0:T(8,128)(2,1)} %copy-done.22, bf16[512,256]{1,0:T(8,128)(2,1)} %copy-done.23, ...), custom_call_target="tpu_custom_call" | custom-call | flops 3489660928 | bytes 4194304 | tf_op jit(solution)/shard_map/pallas_call | solution.py:385
  81.1 6.0 %all-to-all-start.2 = ((bf16[16,96,256]{2,1,0:T(8,128)(2,1)}), bf16[16,96,256]{2,1,0:T(8,128)(2,1)S(1)}, u32[]{:S(2)}, u32[]{:S(2)}) async-start(bf16[16,96,256]{2,1,0:T(8,128)(2,1)} %bitcast.42), calls=%async_computation.2 | async-start | bytes 1572864 | tf_op jit(solution)/shard_map/all_to_all | solution.py:340
  90.5 2.6 %collective-permute-done.14.refs_1_ = bf16[256,256]{1,0:T(8,128)(2,1)S(1)} collective-permute-done((bf16[256,256]{1,0:T(8,128)(2,1)S(1)}, bf16[256,256]{1,0:T(8,128)(2,1)S(1)}, u32[]{:S(2)}, u32[]{:S(2)}) %collective-permute-start.14) | collective-permute-done | bytes 131104 | tf_op jit(solution)/shard_map/ppermute | solution.py:332
  93.1 2.8 %collective-permute-done.15.refs_2_ = bf16[256,256]{1,0:T(8,128)(2,1)S(1)} collective-permute-done((bf16[256,256]{1,0:T(8,128)(2,1)S(1)}, bf16[256,256]{1,0:T(8,128)(2,1)S(1)}, u32[]{:S(2)}, u32[]{:S(2)}) %collective-permute-start.15) | collective-permute-done | bytes 131104 | tf_op jit(solution)/shard_map/ppermute | solution.py:332
  96.3 4.3 %all-to-all-done.2.in_ref = bf16[16,96,256]{2,1,0:T(8,128)(2,1)S(1)} async-done(((bf16[16,96,256]{2,1,0:T(8,128)(2,1)}), bf16[16,96,256]{2,1,0:T(8,128)(2,1)S(1)}, u32[]{:S(2)}, u32[]{:S(2)}) %all-to-all-start.2) | async-done | bytes 786464 | tf_op jit(solution)/shard_map/all_to_all | solution.py:340
  101.7 3.6 %all-to-all-start.3 = ((bf16[16,96,256]{2,1,0:T(8,128)(2,1)}), bf16[16,96,256]{2,1,0:T(8,128)(2,1)S(1)}, u32[]{:S(2)}, u32[]{:S(2)}) async-start(bf16[16,96,256]{2,1,0:T(8,128)(2,1)} %get-tuple-element.72), calls=%async_computation.3 | async-start | bytes 1572864 | tf_op jit(solution)/shard_map/all_to_all | solution.py:340
  110.5 7.6 %all-to-all-done.3 = bf16[16,96,256]{2,1,0:T(8,128)(2,1)S(1)} async-done(((bf16[16,96,256]{2,1,0:T(8,128)(2,1)}), bf16[16,96,256]{2,1,0:T(8,128)(2,1)S(1)}, u32[]{:S(2)}, u32[]{:S(2)}) %all-to-all-start.3) | async-done | bytes 786464 | tf_op jit(solution)/shard_map/all_to_all | solution.py:340
  119.0 13.8 %shard_map.108 = (bf16[544,256]{1,0:T(8,128)(2,1)}, bf16[544,256]{1,0:T(8,128)(2,1)}, bf16[544,256]{1,0:T(8,128)(2,1)}, bf16[544,256]{1,0:T(8,128)(2,1)}, bf16[16,3,32,256]{3,2,1,0:T(8,128)(2,1)}) custom-call(bf16[544,256]{1,0:T(8,128)(2,1)} %copy-done.7, bf16[544,256]{1,0:T(8,128)(2,1)} %copy-done.12, bf16[544,256]{1,0:T(8,128)(2,1)} %copy-done.13, ...), custom_call_target="tpu_custom_call" | custom-call | flops 6442450944 | bytes 4194304 | tf_op jit(solution)/shard_map/pallas_call | solution.py:408
  132.8 3.8 %all-to-all-start.4 = ((bf16[16,96,256]{2,1,0:T(8,128)(2,1)}), bf16[16,96,256]{2,1,0:T(8,128)(2,1)S(1)}, u32[]{:S(2)}, u32[]{:S(2)}) async-start(bf16[16,96,256]{2,1,0:T(8,128)(2,1)} %bitcast.41), calls=%async_computation.4 | async-start | bytes 1572864 | tf_op jit(solution)/shard_map/all_to_all | solution.py:340
  140.0 8.4 %all-to-all-done.4.in_ref = bf16[16,96,256]{2,1,0:T(8,128)(2,1)S(1)} async-done(((bf16[16,96,256]{2,1,0:T(8,128)(2,1)}), bf16[16,96,256]{2,1,0:T(8,128)(2,1)S(1)}, u32[]{:S(2)}, u32[]{:S(2)}) %all-to-all-start.4) | async-done | bytes 786464 | tf_op jit(solution)/shard_map/all_to_all | solution.py:340
  148.5 3.7 %collective-permute-start.28 = (f32[3,16,256]{2,1,0:T(8,128)S(1)}, f32[3,16,256]{2,1,0:T(8,128)S(1)}, u32[]{:S(2)}, u32[]{:S(2)}) collective-permute-start(f32[3,16,256]{2,1,0:T(8,128)S(1)} %dynamic-slice_bitcast_fusion.1), channel_id=1, source_target_pairs={{0,1},{1,0},{2,3},{3,2},{4,5},{5,4},{6,7},{7,6},{8,9},{9,8},{10,11... | collective-permute-start | bytes 147464 | tf_op jit(solution)/shard_map/ppermute | solution.py:429
  (125 shorter events, 39.6 us)
Async XLA Ops:
  4.2 10.9 %collective-permute-start = (bf16[544,256]{1,0:T(8,128)(2,1)S(1)}, bf16[544,256]{1,0:T(8,128)(2,1)S(1)}, u32[]{:S(2)}, u32[]{:S(2)}) collective-permute-start(bf16[544,256]{1,0:T(8,128)(2,1)S(1)} %get-tuple-element.50), channel_id=1, source_target_pairs={{0,64},{32,96},{64,0},{96,32},{1,65},{33,97},{65,1},{97,33},{2,66}... | collective-permute-start | bytes 835592 | tf_op jit(solution)/shard_map/ppermute | solution.py:332
  8.8 13.1 %collective-permute-start.1 = (bf16[544,256]{1,0:T(8,128)(2,1)S(1)}, bf16[544,256]{1,0:T(8,128)(2,1)S(1)}, u32[]{:S(2)}, u32[]{:S(2)}) collective-permute-start(bf16[544,256]{1,0:T(8,128)(2,1)S(1)} %get-tuple-element.51), channel_id=1, source_target_pairs={{0,32},{32,64},{64,96},{96,0},{1,33},{33,65},{65,97},{97,1},{2,34}... | collective-permute-start | bytes 835592 | tf_op jit(solution)/shard_map/ppermute | solution.py:332
  9.5 12.8 %collective-permute-start.2 = (bf16[544,256]{1,0:T(8,128)(2,1)S(1)}, bf16[544,256]{1,0:T(8,128)(2,1)S(1)}, u32[]{:S(2)}, u32[]{:S(2)}) collective-permute-start(bf16[544,256]{1,0:T(8,128)(2,1)S(1)} %get-tuple-element.52), channel_id=1, source_target_pairs={{0,96},{32,0},{64,32},{96,64},{1,97},{33,1},{65,33},{97,65},{2,98}... | collective-permute-start | bytes 835592 | tf_op jit(solution)/shard_map/ppermute | solution.py:332
  11.4 14.8 %collective-permute-start.3 = (bf16[544,256]{1,0:T(8,128)(2,1)S(1)}, bf16[544,256]{1,0:T(8,128)(2,1)S(1)}, u32[]{:S(2)}, u32[]{:S(2)}) collective-permute-start(bf16[544,256]{1,0:T(8,128)(2,1)S(1)} %get-tuple-element.49.refs_0_), channel_id=1, source_target_pairs={{0,1},{1,0},{2,3},{3,2},{4,5},{5,4},{6,7},{7,6},{8,9},{9,8},{10,11... | collective-permute-start | bytes 835592 | tf_op jit(solution)/shard_map/ppermute | solution.py:336
  15.2 11.0 %collective-permute-start.4 = (bf16[544,256]{1,0:T(8,128)(2,1)S(1)}, bf16[544,256]{1,0:T(8,128)(2,1)S(1)}, u32[]{:S(2)}, u32[]{:S(2)}) collective-permute-start(bf16[544,256]{1,0:T(8,128)(2,1)S(1)} %collective-permute-done.refs_1_), channel_id=1, source_target_pairs={{0,1},{1,0},{2,3},{3,2},{4,5},{5,4},{6,7},{7,6},{8,9},{9,8},{10,11... | collective-permute-start | bytes 835592 | tf_op jit(solution)/shard_map/ppermute | solution.py:336
  21.8 4.4 %collective-permute-start.5 = (bf16[544,256]{1,0:T(8,128)(2,1)S(1)}, bf16[544,256]{1,0:T(8,128)(2,1)S(1)}, u32[]{:S(2)}, u32[]{:S(2)}) collective-permute-start(bf16[544,256]{1,0:T(8,128)(2,1)S(1)} %collective-permute-done.1.refs_2_), channel_id=1, source_target_pairs={{0,1},{1,0},{2,3},{3,2},{4,5},{5,4},{6,7},{7,6},{8,9},{9,8},{10,11... | collective-permute-start | bytes 835592 | tf_op jit(solution)/shard_map/ppermute | solution.py:336
  22.3 3.9 %collective-permute-start.6 = (bf16[544,256]{1,0:T(8,128)(2,1)S(1)}, bf16[544,256]{1,0:T(8,128)(2,1)S(1)}, u32[]{:S(2)}, u32[]{:S(2)}) collective-permute-start(bf16[544,256]{1,0:T(8,128)(2,1)S(1)} %collective-permute-done.2.refs_3_), channel_id=1, source_target_pairs={{0,1},{1,0},{2,3},{3,2},{4,5},{5,4},{6,7},{7,6},{8,9},{9,8},{10,11... | collective-permute-start | bytes 835592 | tf_op jit(solution)/shard_map/ppermute | solution.py:336
  34.5 20.7 %all-to-all-start = ((bf16[16,96,256]{2,1,0:T(8,128)(2,1)}), bf16[16,96,256]{2,1,0:T(8,128)(2,1)S(1)}, u32[]{:S(2)}, u32[]{:S(2)}) async-start(bf16[16,96,256]{2,1,0:T(8,128)(2,1)} %bitcast.40), calls=%async_computation | async-start | bytes 1572864 | tf_op jit(solution)/shard_map/all_to_all | solution.py:340
  42.2 9.1 %collective-permute-start.7 = (bf16[512,256]{1,0:T(8,128)(2,1)S(1)}, bf16[512,256]{1,0:T(8,128)(2,1)S(1)}, u32[]{:S(2)}, u32[]{:S(2)}) collective-permute-start(bf16[512,256]{1,0:T(8,128)(2,1)S(1)} %get-tuple-element.54), channel_id=1, source_target_pairs={{0,64},{32,96},{64,0},{96,32},{1,65},{33,97},{65,1},{97,33},{2,66}... | collective-permute-start | bytes 786440 | tf_op jit(solution)/shard_map/ppermute | solution.py:332
  56.4 16.5 %all-to-all-start.1 = ((bf16[16,96,256]{2,1,0:T(8,128)(2,1)}), bf16[16,96,256]{2,1,0:T(8,128)(2,1)S(1)}, u32[]{:S(2)}, u32[]{:S(2)}) async-start(bf16[16,96,256]{2,1,0:T(8,128)(2,1)} %get-tuple-element.59), calls=%async_computation.1 | async-start | bytes 1572864 | tf_op jit(solution)/shard_map/all_to_all | solution.py:340
  60.1 7.7 %collective-permute-start.8 = (bf16[512,256]{1,0:T(8,128)(2,1)S(1)}, bf16[512,256]{1,0:T(8,128)(2,1)S(1)}, u32[]{:S(2)}, u32[]{:S(2)}) collective-permute-start(bf16[512,256]{1,0:T(8,128)(2,1)S(1)} %get-tuple-element.56), channel_id=1, source_target_pairs={{0,32},{32,64},{64,96},{96,0},{1,33},{33,65},{65,97},{97,1},{2,34}... | collective-permute-start | bytes 786440 | tf_op jit(solution)/shard_map/ppermute | solution.py:332
  60.6 9.5 %collective-permute-start.9 = (bf16[512,256]{1,0:T(8,128)(2,1)S(1)}, bf16[512,256]{1,0:T(8,128)(2,1)S(1)}, u32[]{:S(2)}, u32[]{:S(2)}) collective-permute-start(bf16[512,256]{1,0:T(8,128)(2,1)S(1)} %get-tuple-element.57), channel_id=1, source_target_pairs={{0,96},{32,0},{64,32},{96,64},{1,97},{33,1},{65,33},{97,65},{2,98}... | collective-permute-start | bytes 786440 | tf_op jit(solution)/shard_map/ppermute | solution.py:332
  62.8 7.8 %collective-permute-start.10 = (bf16[512,256]{1,0:T(8,128)(2,1)S(1)}, bf16[512,256]{1,0:T(8,128)(2,1)S(1)}, u32[]{:S(2)}, u32[]{:S(2)}) collective-permute-start(bf16[512,256]{1,0:T(8,128)(2,1)S(1)} %get-tuple-element.53.refs_0_), channel_id=1, source_target_pairs={{0,1},{1,0},{2,3},{3,2},{4,5},{5,4},{6,7},{7,6},{8,9},{9,8},{10,11... | collective-permute-start | bytes 786440 | tf_op jit(solution)/shard_map/ppermute | solution.py:336
  67.7 3.5 %collective-permute-start.12 = (bf16[512,256]{1,0:T(8,128)(2,1)S(1)}, bf16[512,256]{1,0:T(8,128)(2,1)S(1)}, u32[]{:S(2)}, u32[]{:S(2)}) collective-permute-start(bf16[512,256]{1,0:T(8,128)(2,1)S(1)} %collective-permute-done.8.refs_2_), channel_id=1, source_target_pairs={{0,1},{1,0},{2,3},{3,2},{4,5},{5,4},{6,7},{7,6},{8,9},{9,8},{10,11... | collective-permute-start | bytes 786440 | tf_op jit(solution)/shard_map/ppermute | solution.py:336
  81.1 19.5 %all-to-all-start.2 = ((bf16[16,96,256]{2,1,0:T(8,128)(2,1)}), bf16[16,96,256]{2,1,0:T(8,128)(2,1)S(1)}, u32[]{:S(2)}, u32[]{:S(2)}) async-start(bf16[16,96,256]{2,1,0:T(8,128)(2,1)} %bitcast.42), calls=%async_computation.2 | async-start | bytes 1572864 | tf_op jit(solution)/shard_map/all_to_all | solution.py:340
  87.1 6.0 %collective-permute-start.14 = (bf16[256,256]{1,0:T(8,128)(2,1)S(1)}, bf16[256,256]{1,0:T(8,128)(2,1)S(1)}, u32[]{:S(2)}, u32[]{:S(2)}) collective-permute-start(bf16[256,256]{1,0:T(8,128)(2,1)S(1)} %copy-done.31), channel_id=1, source_target_pairs={{0,64},{32,96},{64,0},{96,32},{1,65},{33,97},{65,1},{97,33},{2,66}... | collective-permute-start | bytes 393224 | tf_op jit(solution)/shard_map/ppermute | solution.py:332
  89.0 6.8 %collective-permute-start.15 = (bf16[256,256]{1,0:T(8,128)(2,1)S(1)}, bf16[256,256]{1,0:T(8,128)(2,1)S(1)}, u32[]{:S(2)}, u32[]{:S(2)}) collective-permute-start(bf16[256,256]{1,0:T(8,128)(2,1)S(1)} %copy-done.30), channel_id=1, source_target_pairs={{0,96},{32,0},{64,32},{96,64},{1,97},{33,1},{65,33},{97,65},{2,98}... | collective-permute-start | bytes 393224 | tf_op jit(solution)/shard_map/ppermute | solution.py:332
  89.7 6.7 %collective-permute-start.16 = (bf16[256,256]{1,0:T(8,128)(2,1)S(1)}, bf16[256,256]{1,0:T(8,128)(2,1)S(1)}, u32[]{:S(2)}, u32[]{:S(2)}) collective-permute-start(bf16[256,256]{1,0:T(8,128)(2,1)S(1)} %copy-done.29), channel_id=1, source_target_pairs={{0,32},{32,64},{64,96},{96,0},{1,33},{33,65},{65,97},{97,1},{2,34}... | collective-permute-start | bytes 393224 | tf_op jit(solution)/shard_map/ppermute | solution.py:332
  101.7 16.3 %all-to-all-start.3 = ((bf16[16,96,256]{2,1,0:T(8,128)(2,1)}), bf16[16,96,256]{2,1,0:T(8,128)(2,1)S(1)}, u32[]{:S(2)}, u32[]{:S(2)}) async-start(bf16[16,96,256]{2,1,0:T(8,128)(2,1)} %get-tuple-element.72), calls=%async_computation.3 | async-start | bytes 1572864 | tf_op jit(solution)/shard_map/all_to_all | solution.py:340
  132.8 15.5 %all-to-all-start.4 = ((bf16[16,96,256]{2,1,0:T(8,128)(2,1)}), bf16[16,96,256]{2,1,0:T(8,128)(2,1)S(1)}, u32[]{:S(2)}, u32[]{:S(2)}) async-start(bf16[16,96,256]{2,1,0:T(8,128)(2,1)} %bitcast.41), calls=%async_computation.4 | async-start | bytes 1572864 | tf_op jit(solution)/shard_map/all_to_all | solution.py:340
  136.6 15.7 %collective-permute-start.22 = (bf16[544,256]{1,0:T(8,128)(2,1)S(1)}, bf16[544,256]{1,0:T(8,128)(2,1)S(1)}, u32[]{:S(2)}, u32[]{:S(2)}) collective-permute-start(bf16[544,256]{1,0:T(8,128)(2,1)S(1)} %copy-done.21), channel_id=1, source_target_pairs={{0,64},{32,96},{64,0},{96,32},{1,65},{33,97},{65,1},{97,33},{2,66}... | collective-permute-start | bytes 835592 | tf_op jit(solution)/shard_map/ppermute | solution.py:332
  138.5 14.1 %collective-permute-start.24 = (bf16[544,256]{1,0:T(8,128)(2,1)S(1)}, bf16[544,256]{1,0:T(8,128)(2,1)S(1)}, u32[]{:S(2)}, u32[]{:S(2)}) collective-permute-start(bf16[544,256]{1,0:T(8,128)(2,1)S(1)} %copy-done.20), channel_id=1, source_target_pairs={{0,96},{32,0},{64,32},{96,64},{1,97},{33,1},{65,33},{97,65},{2,98}... | collective-permute-start | bytes 835592 | tf_op jit(solution)/shard_map/ppermute | solution.py:332
  139.1 14.1 %collective-permute-start.26 = (bf16[544,256]{1,0:T(8,128)(2,1)S(1)}, bf16[544,256]{1,0:T(8,128)(2,1)S(1)}, u32[]{:S(2)}, u32[]{:S(2)}) collective-permute-start(bf16[544,256]{1,0:T(8,128)(2,1)S(1)} %copy-done.19), channel_id=1, source_target_pairs={{0,32},{32,64},{64,96},{96,0},{1,33},{33,65},{65,97},{97,1},{2,34}... | collective-permute-start | bytes 835592 | tf_op jit(solution)/shard_map/ppermute | solution.py:332
  148.5 4.7 %collective-permute-start.28 = (f32[3,16,256]{2,1,0:T(8,128)S(1)}, f32[3,16,256]{2,1,0:T(8,128)S(1)}, u32[]{:S(2)}, u32[]{:S(2)}) collective-permute-start(f32[3,16,256]{2,1,0:T(8,128)S(1)} %dynamic-slice_bitcast_fusion.1), channel_id=1, source_target_pairs={{0,1},{1,0},{2,3},{3,2},{4,5},{5,4},{6,7},{7,6},{8,9},{9,8},{10,11... | collective-permute-start | bytes 147464 | tf_op jit(solution)/shard_map/ppermute | solution.py:429
  (42 other events, 244.3 us)
